TPU v7x, 128 devices: a whole 4x4x4 slice. The times are simulated.
128 devices in a mesh: dp: 4 (over z), ctx: 32 (over y, x, core).
Axes of the slice: x: 4, y: 4, z: 4, core: 2. Of those that a mesh axis runs over, the one named last changes fastest.
Arguments:
- streams: bfloat16 [32768, 12288], P(('dp', 'ctx')), parts along dimension 0, may hold values from -6 to 6
- short_filter: float32 [3, 12288], replicated, may hold values from -3 to 3
- rates: float32 [256, 16], replicated, may hold values from 6.1035156e-05 to 0.03
- residues: float32 [256, 16], replicated, may hold values from -3 to 3
- skip: float32 [4096], replicated, may hold values from -4 to 4
Outputs:
- gated: float32 [32768, 4096], P(('dp', 'ctx')), parts along dimension 0
There are 4 independent parts, one for each index of `dp`. A program takes and returns all parts, laid end to end along the dimension named above; an argument that names none is the same for every part. Nothing has to cross between parts.
All inputs are finite; a program needn't handle non-finite values.
Results may differ from a plain program's by a relative error of at most 0.0003.
Values may be sent and summed in bfloat16 or wider, within the bound.
A program may use at most 320 MiB of HBM per device.

v0:
```python
import jax
import jax.numpy as jnp
from jax import lax
from jax.sharding import PartitionSpec as P


def passed_along(block, axis, distance):
    devices = range(lax.axis_size(axis))
    route = [(i - distance, i) for i in devices if i - distance in devices]
    return lax.ppermute(block, axis, route)


def prefix(array, axis, combine, identity):
    count, here = (lax.axis_size(axis), lax.axis_index(axis))
    everything = jax.tree.map(lambda part: lax.all_gather(part, axis), array)
    start = jax.tree.map(
        lambda part, zero: jnp.broadcast_to(jnp.asarray(zero, part.dtype), part.shape),
        array,
        identity,
    )

    def turn(k, before):
        reached = k < here
        new = combine(before, jax.tree.map(lambda part: part[k], everything))
        return jax.tree.map(lambda a, b: jnp.where(reached, a, b), new, before)

    return lax.fori_loop(0, count, turn, start)


def combine_states(earlier, later):
    return (earlier[0] * later[1][:, :, None] + later[0], earlier[1] * later[1])


def body(streams, short_filter, rates, residues, skip):
    rows = streams.shape[0]
    channels = skip.shape[0]
    groups, order = rates.shape
    group_size = channels // groups
    width = short_filter.shape[0] - 1
    rim = passed_along(streams[rows - width :], "ctx", 1)
    zpad = jnp.concatenate([rim, streams], axis=0).astype(jnp.float32)
    feat = jnp.zeros((rows, streams.shape[1]), jnp.float32)
    for tap in range(width + 1):
        feat = feat + short_filter[tap][None, :] * zpad[width - tap : width - tap + rows]
    query = feat[:, :channels]
    key_part = feat[:, channels : 2 * channels]
    value = feat[:, 2 * channels :]
    inner = key_part * value
    amp = residues * -jnp.expm1(-rates)
    block = min(rows, 128)
    count_blocks = rows // block
    lags = jnp.arange(block).astype(jnp.float32)
    taps = jnp.sum(jnp.exp(-lags[:, None, None] * rates[None, :, :]) * amp[None, :, :], axis=2).T
    padded_taps = jnp.concatenate([jnp.zeros((groups, block - 1), jnp.float32), taps], axis=1)
    reversed_taps = padded_taps[:, ::-1]
    rolled = jnp.concatenate([reversed_taps[:, block - 1 :], reversed_taps[:, : block - 1]], axis=1)
    period = 2 * block - 1
    tiled = jnp.tile(rolled, (1, block))[:, : block * (period - 1)]
    toeplitz = tiled.reshape(groups, block, period - 1)[:, :, :block]
    inner_blocks = inner.reshape(count_blocks, block, groups, group_size)
    lanes = inner_blocks.transpose(2, 1, 0, 3).reshape(groups, block, count_blocks * group_size)
    local = jnp.einsum("gts,gsm->gmt", toeplitz, lanes, precision=lax.Precision.HIGH)
    local = local.reshape(groups, count_blocks, group_size, block).transpose(1, 3, 0, 2)
    backward = jnp.exp(-(block - 1.0 - lags)[:, None, None] * rates[None, :, :])
    block_sums = jnp.einsum("sgn,ksgc->kgnc", backward, inner_blocks, precision=lax.Precision.HIGH)
    step_decay = jnp.exp(-rates * block)
    summary = jnp.zeros((groups, order, group_size), jnp.float32)
    for index in range(count_blocks):
        summary = summary * step_decay[:, :, None] + block_sums[index]
    block_decay = jnp.exp(-rates * rows)
    identity = (jnp.zeros_like(summary), jnp.ones_like(block_decay))
    incoming, unused_decay = prefix((summary, block_decay), "ctx", combine_states, identity)
    states = []
    state = incoming
    for index in range(count_blocks):
        states.append(state)
        state = state * step_decay[:, :, None] + block_sums[index]
    states = jnp.stack(states, axis=0)
    forward = jnp.exp(-(lags + 1.0)[:, None, None] * rates[None, :, :]) * amp[None, :, :]
    carried = jnp.einsum("tgn,kgnc->ktgc", forward, states, precision=lax.Precision.HIGH)
    conv = (local + carried).reshape(rows, channels)
    return query * (conv + skip[None, :] * inner)


def solution(mesh):
    in_specs = (P(("dp", "ctx"), None), P(), P(), P(), P())
    out_specs = P(("dp", "ctx"), None)
    return jax.shard_map(body, mesh=mesh, in_specs=in_specs, out_specs=out_specs, check_vma=False)
```

profile of v0, /device:TPU:1, one launch (start us, length us, event | category | flops | bytes accessed | tf_op | source)
XLA Modules:
  0.0 394.7 jit_solution(16718714443293069254)
XLA Ops:
  7.5 4.5 %collective-permute-start = (bf16[2,12288]{1,0:T(2,128)(2,1)S(1)}, bf16[2,12288]{1,0:T(2,128)(2,1)}, u32[]{:S(2)}, u32[]{:S(2)}) collective-permute-start(bf16[2,12288]{1,0:T(2,128)(2,1)S(1)} %slice.57), channel_id=1, source_target_pairs={{0,1},{1,2},{2,3},{3,4},{4,5},{5,6},{6,7},{7,8},{8,9},{9,10},{10,1... | collective-permute-start | bytes 147464 | tf_op jit(solution)/shard_map/ppermute | solution.py:10
  12.0 1.9 fusion.28
  13.9 1.4 broadcast_multiply_fusion.1
  15.8 8.6 %copy.69 = bf16[256,12288]{0,1:T(8,128)(2,1)} copy(bf16[256,12288]{1,0:T(8,128)(2,1)} %param.7) | data formatting | bytes 12582912 | tf_op args[0]
  24.8 2.5 copy.68
  27.3 5.9 %maximum_convert_fusion = f32[258,12288]{0,1:T(8,128)S(1)} fusion(bf16[256,12288]{0,1:T(8,128)(2,1)} %copy.69, bf16[2,12288]{0,1:T(8,128)(2,1)S(1)} %copy.68), kind=kLoop, calls=%fused_computation.11 | loop fusion | flops 12681216 | bytes 19021824 | tf_op jit(solution)/shard_map/convert_element_type | solution.py:41
  33.2 12.8 %fusion.3 = f32[256,12288]{0,1:T(8,128)S(1)} fusion(f32[258,12288]{0,1:T(8,128)S(1)} %maximum_convert_fusion, f32[12288]{0:T(1024)S(1)} %bitcast.67, f32[12288]{0:T(1024)S(1)} %bitcast.68, f32[12288]{0:T(1024)S(1)} %bitcast.66), kind=kLoop, calls=%fused_computation.7 | loop fusion | flops 15728640 | bytes 50479104 | tf_op jit(solution)/shard_map/add | solution.py:44
  46.0 4.5 %copy-done = f32[256,12288]{0,1:T(8,128)} copy-done((f32[256,12288]{0,1:T(8,128)}, f32[256,12288]{0,1:T(8,128)S(1)}, u32[]{:S(2)}) %copy-start) | copy-done | bytes 12582936
  50.5 2.6 slice_multiply_fusion.3
  53.1 5.8 %reshape.40 = f32[2,128,256,16]{1,0,3,2:T(2,128)} reshape(f32[256,4096]{0,1:T(8,128)} %slice_multiply_fusion.3) | data formatting | bytes 8388608 | tf_op jit(solution)/shard_map/reshape | solution.py:60
  58.8 4.3 %fusion.10 = f32[2,256,16,16]{2,3,0,1:T(8,128)S(1)} fusion(f32[2,128,256,16]{1,0,3,2:T(2,128)} %reshape.40, f32[128]{0:T(128)S(1)} %copy-done.9, f32[256,16]{1,0:T(8,128)S(1)} %copy.71), kind=kOutput, calls=%fused_computation.21 | convolution fusion | flops 101187584 | bytes 4735488 | tf_op jit(solution)/shard_map/sgn,ksgc->kgnc/dot_general | solution.py:65
  63.2 1.9 copy-done.1
  65.1 1.9 slice_add_fusion
  67.1 24.0 %all-gather = f32[8192,16]{0,1:T(8,128)S(1)} all-gather(f32[256,16]{0,1:T(8,128)S(1)} %copy-done.7), channel_id=2, replica_groups=mesh['dp'=4,'ctx'=32] {'ctx'}, dimensions={0}, use_global_device_ids=true | all-gather | bytes 540672 | tf_op jit(solution)/shard_map/all_gather | solution.py:15
  91.4 1.9 multiply_reduce_fusion
  93.8 11.4 %tile.4 = f32[256,128,255]{2,1,0:T(8,128)} broadcast(f32[256,255]{1,0:T(8,128)S(1)} %pad_maximum_fusion.1), dimensions={0,2} | broadcast | bytes 33684480 | tf_op jit(solution)/shard_map/tile | solution.py:58
  105.2 34.1 %tile.10 = f32[256,32640]{1,0:T(8,128)} reshape(f32[256,128,255]{2,1,0:T(8,128)} %tile.4) | data formatting | bytes 66846720 | tf_op jit(solution)/shard_map/tile | solution.py:58
  139.3 23.1 %slice.81 = f32[256,32512]{1,0:T(8,128)} slice(f32[256,32640]{1,0:T(8,128)} %tile.10), slice={[0:256], [0:32512]} | slice | bytes 66584576 | tf_op jit(solution)/shard_map/slice | solution.py:58
  162.4 54.0 %reshape.42 = f32[256,128,254]{2,1,0:T(8,128)} reshape(f32[256,32512]{1,0:T(8,128)} %slice.81) | data formatting | bytes 66584576 | tf_op jit(solution)/shard_map/reshape | solution.py:59
  216.4 2.6 copy.70
  219.1 17.1 %fusion.1 = f32[256,32,128]{2,1,0:T(8,128)} fusion(f32[256,128,32]{1,2,0:T(8,128)S(1)} %bitcast.58, f32[256,128,254]{2,1,0:T(8,128)} %reshape.42), kind=kOutput, calls=%fused_computation.4 | convolution fusion | flops 805306368 | bytes 25165824 | tf_op jit(solution)/shard_map/gts,gsm->gmt/dot_general | solution.py:62
  236.2 50.8 %all-gather.3.cloned.1.call-done = f32[32,256,16,16]{2,3,0,1:T(8,128)} async-done(((f32[1,256,16,16]{2,3,0,1:T(8,128)}), f32[32,256,16,16]{2,3,0,1:T(8,128)}) %all-gather.3.cloned.1.call-update) | async-done | bytes 8388624 | tf_op jit(solution)/shard_map/all_gather | solution.py:15
  287.0 38.8 %copy.77 = f32[32,256,16,16]{1,3,2,0:T(8,128)} copy(f32[32,256,16,16]{2,3,0,1:T(8,128)} %all-gather.3.cloned.1.call-done) | data formatting | bytes 16777216
  325.8 39.3 %while.14 = (s32[]{:T(128)}, f32[256,16,16]{0,2,1:T(8,128)S(1)}, s32[]{:T(128)}, f32[32,256,16]{1,0,2:T(8,128)S(1)}, f32[32,256,16,16]{1,3,2,0:T(8,128)}, /*index=5*/s32[]{:T(128)}, s32[]{:T(128)}) while((s32[]{:T(128)}, f32[256,16,16]{0,2,1:T(8,128)S(1)}, s32[]{:T(128)}, f32[32,256,16]{1,0,2:T(8,128)S(1)}, ...), condition=%wide.region_2.3_spmd.clone, body=%wide.region_1.2_spmd.clone.sunk | while | flops 262148 | bytes 868457 | solution.py:27
  325.9 1.2 fusion.31
  327.1 1.2 fusion.31
  328.3 1.2 fusion.31
  330.8 1.2 fusion.31
  332.0 1.2 fusion.31
  334.5 1.2 fusion.31
  335.7 1.2 fusion.31
  338.2 1.2 fusion.31
  339.4 1.2 fusion.31
  341.8 1.2 fusion.31
  343.1 1.2 fusion.31
  345.5 1.2 fusion.31
  346.8 1.2 fusion.31
  348.0 1.2 fusion.31
  349.2 1.2 fusion.31
  350.5 1.2 fusion.31
  351.7 1.2 fusion.31
  365.2 1.3 copy.78
  366.5 2.5 copy.81
  369.0 2.7 fusion.17
  371.8 5.7 %add_bitcast_fusion = f32[2,128,256,16]{1,3,0,2:T(8,128)S(1)} fusion(f32[256,2,16,128]{3,2,1,0:T(8,128)} %bitcast.57, f32[128]{0:T(128)S(1)} %add_negate_fusion, f32[256,16]{1,0:T(8,128)S(1)} %copy.72, f32[256,16]{1,0:T(8,128)S(1)} %copy.71, f32[1,256,16,16]{2,3,1,0:T(8,128)S(1)} %fusion.17, f32[1,256,16,16]{2,3,1,0:T(8,128)S(1)} %bitcast.60), kind=kOutput, calls=%fused_computation.20 | convolution fusion | flops 102891520 | bytes 8946176 | tf_op jit(solution)/shard_map/tgn,kgnc->ktgc/dot_general | solution.py:80
  377.5 2.2 copy.83
  379.7 2.5 fusion.5
  382.2 5.6 %copy.84 = f32[256,4096]{1,0:T(8,128)} copy(f32[256,4096]{0,1:T(8,128)} %fusion.5) | data formatting | bytes 8388608 | tf_op jit(solution)/shard_map/mul | solution.py:82
  (123 shorter events, 21.0 us)
Async XLA Ops:
  6.5 280.4 %all-gather.3.cloned.1.call-start = ((), (), s32[]{:S(2)}) async-start(), calls=%async_computation | async-start | bytes 69206016 | tf_op jit(solution)/shard_map/all_gather | solution.py:15
  7.5 17.3 %collective-permute-start = (bf16[2,12288]{1,0:T(2,128)(2,1)S(1)}, bf16[2,12288]{1,0:T(2,128)(2,1)}, u32[]{:S(2)}, u32[]{:S(2)}) collective-permute-start(bf16[2,12288]{1,0:T(2,128)(2,1)S(1)} %slice.57), channel_id=1, source_target_pairs={{0,1},{1,2},{2,3},{3,4},{4,5},{5,6},{6,7},{7,8},{8,9},{9,10},{10,1... | collective-permute-start | bytes 147464 | tf_op jit(solution)/shard_map/ppermute | solution.py:10
  15.8 8.7 %copy-start.5 = (f32[256,16]{0,1:T(8,128)S(1)}, f32[256,16]{0,1:T(8,128)}, u32[]{:S(2)}) copy-start(f32[256,16]{0,1:T(8,128)} %param.9) | copy-start | bytes 49156
  27.3 5.9 %copy-start.2 = (f32[1,12288]{1,0:T(1,128)S(1)}, f32[1,12288]{1,0:T(1,128)}, u32[]{:S(2)}) copy-start(f32[1,12288]{1,0:T(1,128)} %get-tuple-element.153) | copy-start | bytes 147460
  27.3 5.9 %copy-start.3 = (f32[1,12288]{1,0:T(1,128)S(1)}, f32[1,12288]{1,0:T(1,128)}, u32[]{:S(2)}) copy-start(f32[1,12288]{1,0:T(1,128)} %get-tuple-element.154) | copy-start | bytes 147460
  27.3 5.9 %copy-start.4 = (f32[1,12288]{1,0:T(1,128)S(1)}, f32[1,12288]{1,0:T(1,128)}, u32[]{:S(2)}) copy-start(f32[1,12288]{1,0:T(1,128)} %get-tuple-element.155) | copy-start | bytes 147460
  46.0 4.5 %copy-start = (f32[256,12288]{0,1:T(8,128)}, f32[256,12288]{0,1:T(8,128)S(1)}, u32[]{:S(2)}) copy-start(f32[256,12288]{0,1:T(8,128)S(1)} %fusion.3) | copy-start | bytes 37748740
  53.1 5.8 %copy-start.9 = (f32[128]{0:T(128)S(1)}, f32[128]{0:T(128)}, u32[]{:S(2)}) copy-start(f32[128]{0:T(128)} %subtract_negate_fusion) | copy-start | bytes 1540
  63.2 1.9 copy-start.1
  65.1 1.9 copy-start.7
  65.1 26.1 %copy-start.6 = (f32[256,16]{0,1:T(8,128)S(1)}, f32[256,16]{0,1:T(8,128)}, u32[]{:S(2)}) copy-start(f32[256,16]{0,1:T(8,128)} %get-tuple-element.159) | copy-start | bytes 49156
  369.0 10.6 %slice-start = ((s8[12582912]{0:T(1024)(128)(4,1)}), s8[4194304]{0:T(1024)(128)(4,1)S(1)}, s32[]{:S(2)}) async-start(s8[12582912]{0:T(1024)(128)(4,1)} %bitcast.54), calls=%async_computation.1 | async-start | bytes 8388608
  371.7 8.0 %slice-start.1 = ((s8[12582912]{0:T(1024)(128)(4,1)}), s8[4194304]{0:T(1024)(128)(4,1)S(1)}, s32[]{:S(2)}) async-start(s8[12582912]{0:T(1024)(128)(4,1)} %bitcast.54), calls=%async_computation.2 | async-start | bytes 8388608
  371.7 8.0 %slice-start.2 = ((s8[12582912]{0:T(1024)(128)(4,1)}), s8[4194304]{0:T(1024)(128)(4,1)S(1)}, s32[]{:S(2)}) async-start(s8[12582912]{0:T(1024)(128)(4,1)} %bitcast.54), calls=%async_computation.3 | async-start | bytes 8388608
  377.5 2.2 copy-start.8
Sparse Core Ops, SparseCore 0:
  67.2 219.7 all-gather.2
where the time goes:
time: 397 us; the launch traced here: 395 us
  local copies, waits for them, and re-layouts  204 us (51%)
  other arithmetic  69.4 us (17%)
  waiting for transfers between devices  50.8 us (13%)
  matrix products  27.2 us (7%)
  blocking collectives  24 us (6%)
  between operations  13.7 us (3%)
  starting transfers between devices  4.51 us (1%)
    unnamed x30, local copies, waits for them, and re-layouts  54.3 us
    reshape x1, local copies, waits for them, and re-layouts, body(): toeplitz = tiled.reshape(groups, block, period - 1)[:, :, :block]  54 us
    all_gather x1, waiting for transfers between devices, prefix(): everything = jax.tree.map(lambda part: lax.all_gather(part, axis), array)  50.8 us
    another operation x2, local copies, waits for them, and re-layouts, body(): tiled = jnp.tile(rolled, (1, block))[:, :block * (period - 1)]  45.5 us
    select_n x32, other arithmetic, turn(): return jax.tree.map(lambda a, b: jnp.where(reached, a, b), new, before)  37.4 us
    all_gather x1, blocking collectives, prefix(): everything = jax.tree.map(lambda part: lax.all_gather(part, axis), array)  24 us
    slice x1, local copies, waits for them, and re-layouts, body(): tiled = jnp.tile(rolled, (1, block))[:, :block * (period - 1)]  23.1 us
    dot_general x1, matrix products, body(): jnp.einsum('gts,gsm->gmt', toeplitz, lanes, precision=lax.Precision.HIGH)  17.1 us
  transfers between devices with their start and end apart: 2, of which 1 were waited for; matrix products, arithmetic and copies ran while one was open for 40% of the time, Pallas kernels for 0%

commit v1 on v0

v1 whole, which is shorter than its diff:
```python
import functools

import jax
import jax.numpy as jnp
from jax import lax
from jax.experimental import pallas as pl
from jax.experimental.pallas import tpu as pltpu
from jax.sharding import PartitionSpec as P

F32 = jnp.float32
BF16 = jnp.bfloat16
LANES = 128
BLOCK = 16
SPAN = 2 * BLOCK
PER_CHUNK = 4
WIDE = PER_CHUNK * LANES


def halves(x):
    high = x.astype(BF16)
    return high, (x - high.astype(F32)).astype(BF16)


def group_mask():
    row = lax.broadcasted_iota(jnp.int32, (LANES, LANES), 0) // BLOCK
    lane = lax.broadcasted_iota(jnp.int32, (LANES, LANES), 1) // BLOCK
    return row == lane


def spread(mask, x):
    return jnp.where(mask, jnp.concatenate([x] * (LANES // BLOCK), axis=0), jnp.zeros((), BF16))


def paired(mask, first, second):
    first, second = halves(first), halves(second)
    left = jnp.concatenate([spread(mask, first[0]), spread(mask, first[1])], axis=0)
    right = jnp.concatenate([spread(mask, second[0]), spread(mask, second[1])], axis=0)
    return jnp.concatenate([left, right], axis=1)


def stack_rows(parts):
    rows = []
    for part, is_low in parts:
        other = jnp.zeros_like(part) if is_low else part
        rows.append(jnp.concatenate([part, other], axis=1))
    return jnp.concatenate(rows, axis=0)


def main_kernel(
    count, streams, taps, rate, amp, skip,
    loc, query, local_states, decay, forward, incoming,
    xs, last, rim_out, rim_in, weights, shifted, sums_out, sums_in, back_out, back_in,
    stream_sem, last_sem, rim_sems, sums_send, sums_recv, back_send, back_recv,
):
    rows = loc.shape[0]
    channels = loc.shape[1]
    tiles = channels // LANES
    chunks = tiles // PER_CHUNK
    blocks = rows // BLOCK
    me = lax.axis_index("ctx")

    def stream_copy(s, c):
        return pltpu.make_async_copy(
            streams.at[:, pl.ds(pl.multiple_of(s * channels + c * WIDE, WIDE), WIDE)],
            xs.at[s, c], stream_sem.at[s, c])

    def chunk_at(k):
        return lax.rem(me // PER_CHUNK + 1 + k, chunks)

    last_copy = pltpu.make_async_copy(streams.at[pl.ds(rows - BLOCK, BLOCK), :], last, last_sem)
    last_copy.start()

    @pl.loop(0, chunks)
    def _(k):
        c = chunk_at(k)
        stream_copy(1, c).start()
        stream_copy(2, c).start()

    barrier = pltpu.get_barrier_semaphore()

    @pl.loop(1, count)
    def _(i):
        pl.semaphore_signal(barrier, inc=1, device_id={"ctx": lax.rem(me + i, count)},
                            device_id_type=pl.DeviceIdType.MESH)

    last_copy.wait()

    @pl.loop(0, 3 * chunks)
    def _(e):
        for p in range(PER_CHUNK):
            lane = pl.ds(pl.multiple_of(e * WIDE + p * LANES, LANES), LANES)
            rim_out[e, 2 * p:2 * p + 2, :] = last[:, lane].astype(F32)[BLOCK - 2:]

    pl.semaphore_wait(barrier, count - 1)
    rim_copy = pltpu.make_async_remote_copy(
        src_ref=rim_out, dst_ref=rim_in, send_sem=rim_sems.at[0], recv_sem=rim_sems.at[1],
        device_id={"ctx": lax.rem(me + 1, count)}, device_id_type=pl.DeviceIdType.MESH)
    rim_copy.start()

    @pl.loop(0, chunks)
    def _(k):
        stream_copy(0, chunk_at(k)).start()

    @pl.loop(0, tiles)
    def _(t):
        lane = pl.ds(pl.multiple_of(t * LANES, LANES), LANES)
        r = rate[:, lane]
        a = amp[:, lane]
        inside = lax.broadcasted_iota(jnp.int32, (BLOCK, LANES), 1) % BLOCK
        row = lax.broadcasted_iota(jnp.int32, (BLOCK, LANES), 0)
        gap = (row - inside).astype(F32)
        near = jnp.zeros((BLOCK, LANES), F32)
        far = jnp.zeros((BLOCK, LANES), F32)
        step = jnp.exp(-float(BLOCK) * r)
        for n in range(BLOCK):
            one = a[n:n + 1] * jnp.exp(-r[n:n + 1] * gap)
            near = near + one
            far = far + one * step[n:n + 1]
        near = halves(jnp.where(row >= inside, near, 0.0))
        far = halves(far)
        back = halves(jnp.exp(-r * (BLOCK - 1.0 - inside.astype(F32))))
        weights[t] = stack_rows([(far[0], False), (far[1], True), (near[0], False), (back[0], False),
                                 (near[1], True), (back[1], True)])
        decay[:, lane] = jnp.exp(-float(SPAN) * r)
        own = row == inside
        r_own = jnp.sum(jnp.where(own, r, 0.0), axis=0, keepdims=True)
        a_own = jnp.sum(jnp.where(own, a, 0.0), axis=0, keepdims=True)
        out = lax.broadcasted_iota(jnp.int32, (SPAN, LANES), 0).astype(F32) + 1.0
        out = halves(a_own * jnp.exp(-r_own * out))
        forward[t] = stack_rows([(out[0], False), (out[1], True)])

    rim_copy.wait()
    first = jnp.where(me > 0, 1.0, 0.0)

    def shifted_rows(slot, s, c, j):
        lane = pl.ds(pl.multiple_of(j * LANES, LANES), LANES)
        shifted[slot, pl.ds(6, 2), :] = rim_in[s * chunks + c, pl.ds(2 * j, 2), :] * first
        for b in range(blocks):
            shifted[slot, pl.ds(8 + BLOCK * b, BLOCK), :] = xs[s, c, pl.ds(BLOCK * b, BLOCK), lane].astype(F32)

    def filtered(slot, s, t, b):
        lane = pl.ds(pl.multiple_of(s * channels + t * LANES, LANES), LANES)
        total = taps[0:1, lane] * shifted[slot, pl.ds(8 + BLOCK * b, BLOCK), :]
        for tap in (1, 2):
            total = total + taps[tap:tap + 1, lane] * shifted[slot, pl.ds(8 + BLOCK * b - tap, BLOCK), :]
        return total

    def sums_copy(t):
        return pltpu.make_async_remote_copy(
            src_ref=sums_out.at[t], dst_ref=sums_in.at[me], send_sem=sums_send.at[t], recv_sem=sums_recv.at[me],
            device_id={"ctx": t}, device_id_type=pl.DeviceIdType.MESH)

    mask = group_mask()

    @pl.loop(0, chunks)
    def _(k):
        c = chunk_at(k)
        stream_copy(1, c).wait()
        stream_copy(2, c).wait()

        @pl.loop(0, PER_CHUNK)
        def _(i):
            j = lax.rem(me + 1 + i, PER_CHUNK)
            t = c * PER_CHUNK + j
            lane = pl.ds(pl.multiple_of(t * LANES, LANES), LANES)
            shifted_rows(0, 1, c, j)
            shifted_rows(1, 2, c, j)
            step = jnp.exp(-float(BLOCK) * rate[:, lane])
            direct = skip[0:1, lane]
            state = jnp.zeros((BLOCK, LANES), F32)
            for quad in range(blocks // 4):
                inner = [filtered(0, 1, t, 4 * quad + b) * filtered(1, 2, t, 4 * quad + b) for b in range(4)]
                even = jnp.dot(weights[t], paired(mask, inner[0], inner[2]), preferred_element_type=F32)
                odd = jnp.dot(weights[t, 2 * BLOCK:, :], paired(mask, inner[1], inner[3]), preferred_element_type=F32)
                for b in range(4):
                    side = slice((b // 2) * LANES, (b // 2 + 1) * LANES)
                    part = odd[:, side] if b % 2 else even[2 * BLOCK:, side]
                    value = direct * inner[b] + (part[:BLOCK] + part[2 * BLOCK:3 * BLOCK])
                    if b % 2:
                        value = value + (even[:BLOCK, side] + even[BLOCK:2 * BLOCK, side])
                    else:
                        local_states[(4 * quad + b) // 2, :, lane] = state
                    loc[pl.ds((4 * quad + b) * BLOCK, BLOCK), lane] = value
                    state = state * step + (part[BLOCK:2 * BLOCK] + part[3 * BLOCK:])

            @pl.when(t != me)
            def _():
                sums_out[t] = state
                sums_copy(t).start()

            @pl.when(t == me)
            def _():
                sums_in[me] = state

    @pl.loop(0, chunks)
    def _(k):
        c = chunk_at(k)
        stream_copy(0, c).wait()

        @pl.loop(0, PER_CHUNK)
        def _(j):
            t = c * PER_CHUNK + j
            lane = pl.ds(pl.multiple_of(t * LANES, LANES), LANES)
            shifted_rows(0, 0, c, j)
            for b in range(blocks):
                query[pl.ds(b * BLOCK, BLOCK), lane] = filtered(0, 0, t, b)

    def sums_arrival(d):
        return pltpu.make_async_remote_copy(
            src_ref=sums_out.at[d], dst_ref=sums_in.at[d], send_sem=sums_send.at[d], recv_sem=sums_recv.at[d],
            device_id={"ctx": d}, device_id_type=pl.DeviceIdType.MESH)

    def back_copy(d):
        return pltpu.make_async_remote_copy(
            src_ref=back_out.at[d], dst_ref=back_in.at[me], send_sem=back_send.at[d], recv_sem=back_recv.at[me],
            device_id={"ctx": d}, device_id_type=pl.DeviceIdType.MESH)

    def back_arrival(d):
        return pltpu.make_async_remote_copy(
            src_ref=back_out.at[d], dst_ref=back_in.at[d], send_sem=back_send.at[d], recv_sem=back_recv.at[d],
            device_id={"ctx": d}, device_id_type=pl.DeviceIdType.MESH)

    own_lane = pl.ds(pl.multiple_of(me * LANES, LANES), LANES)
    device_decay = jnp.exp(-float(rows) * rate[:, own_lane])

    def turn(d, before):
        @pl.when(d != me)
        def _():
            sums_arrival(d).wait_recv()
            back_out[d] = before
            back_copy(d).start()

        @pl.when(d == me)
        def _():
            back_in[me] = before

        return before * device_decay + sums_in[d]

    lax.fori_loop(0, count, turn, jnp.zeros((BLOCK, LANES), F32))

    @pl.loop(1, count)
    def _(i):
        d = lax.rem(me + i, count)
        back_arrival(d).wait_recv()
        sums_arrival(d).wait_send()
        back_copy(d).wait_send()

    for t in range(tiles):
        incoming[:, t * LANES:(t + 1) * LANES] = back_in[t]


def last_kernel(loc, query, local_states, decay, forward, incoming, out):
    step = pl.program_id(0)
    wide = out.shape[1]
    rows = out.shape[0]
    mask = group_mask()

    @pl.loop(0, wide // LANES)
    def _(j):
        t = step * (wide // LANES) + j
        lane = pl.ds(pl.multiple_of(t * LANES, LANES), LANES)
        here = pl.ds(pl.multiple_of(j * LANES, LANES), LANES)
        carried = incoming[:, lane]
        fade = decay[:, lane]
        for pair in range(rows // SPAN // 2):
            states = []
            for m in (2 * pair, 2 * pair + 1):
                states.append(local_states[m, :, lane] + carried)
                carried = carried * fade
            both = jnp.dot(forward[t], paired(mask, *states), preferred_element_type=F32)
            for side in range(2):
                at = pl.ds((2 * pair + side) * SPAN, SPAN)
                value = both[:, side * LANES:(side + 1) * LANES]
                out[at, here] = query[at, lane] * (loc[at, lane] + (value[:SPAN] + value[SPAN:]))


def body(count, streams, short_filter, rates, residues, skip):
    rows = streams.shape[0]
    channels = skip.shape[0]
    tiles = channels // LANES
    chunks = tiles // PER_CHUNK
    rate = jnp.repeat(rates.T, BLOCK, axis=1)
    amp = jnp.repeat((residues * -jnp.expm1(-rates)).T, BLOCK, axis=1)
    vmem = pl.BlockSpec(memory_space=pltpu.VMEM)
    shapes = (
        ((rows, channels), F32),
        ((rows, channels), F32),
        ((rows // SPAN, BLOCK, channels), F32),
        ((BLOCK, channels), F32),
        ((tiles, 2 * SPAN, 2 * LANES), BF16),
        ((BLOCK, channels), F32),
    )
    parts = pl.pallas_call(
        functools.partial(main_kernel, count),
        out_shape=tuple(pltpu.VMEM(shape, dtype) for shape, dtype in shapes),
        in_specs=[pl.BlockSpec(memory_space=pl.ANY)] + [vmem] * 4,
        out_specs=(vmem,) * len(shapes),
        scratch_shapes=[
            pltpu.VMEM((3, chunks, rows, WIDE), BF16),
            pltpu.VMEM((BLOCK, 3 * channels), BF16),
            pltpu.VMEM((3 * chunks, 8, LANES), F32),
            pltpu.VMEM((3 * chunks, 8, LANES), F32),
            pltpu.VMEM((tiles, 6 * BLOCK, 2 * LANES), BF16),
            pltpu.VMEM((2, rows + 8, LANES), F32),
            pltpu.VMEM((count, BLOCK, LANES), F32),
            pltpu.VMEM((count, BLOCK, LANES), F32),
            pltpu.VMEM((count, BLOCK, LANES), F32),
            pltpu.VMEM((count, BLOCK, LANES), F32),
            pltpu.SemaphoreType.DMA((3, chunks)),
            pltpu.SemaphoreType.DMA,
            pltpu.SemaphoreType.DMA((2,)),
            pltpu.SemaphoreType.DMA((count,)),
            pltpu.SemaphoreType.DMA((count,)),
            pltpu.SemaphoreType.DMA((count,)),
            pltpu.SemaphoreType.DMA((count,)),
        ],
        compiler_params=pltpu.CompilerParams(
            collective_id=0, has_side_effects=True, vmem_limit_bytes=24 << 20),
        name="local_part",
    )(streams, short_filter, rate, amp, skip[None, :])
    parts = [pltpu.with_memory_space_constraint(part, pltpu.VMEM) for part in parts]
    return pl.pallas_call(
        last_kernel,
        grid=(chunks,),
        out_shape=jax.ShapeDtypeStruct((rows, channels), F32),
        in_specs=[vmem] * len(parts),
        out_specs=pl.BlockSpec((rows, WIDE), lambda i: (0, i)),
        compiler_params=pltpu.CompilerParams(vmem_limit_bytes=12 << 20),
        name="carried_part",
    )(*parts)


def solution(mesh):
    count = mesh.shape["ctx"]
    in_specs = (P(("dp", "ctx"), None), P(), P(), P(), P())
    out_specs = P(("dp", "ctx"), None)
    return jax.shard_map(functools.partial(body, count), mesh=mesh, in_specs=in_specs, out_specs=out_specs,
                         check_vma=False)
```

time: 397 us -> 47.8 us (0.12)
  local copies, waits for them, and re-layouts: 204 us -> 7.11 us
  other arithmetic: 69.4 us -> 0.81 us
  waiting for transfers between devices: 50.8 us -> 0 us
  Pallas kernels: 0 us -> 39.6 us
  matrix products: 27.2 us -> 0 us
  blocking collectives: 24 us -> 0 us
  between operations: 13.7 us -> 0.05 us
  starting transfers between devices: 4.51 us -> 0 us
    reshape x2, local copies, waits for them, and re-layouts: 59.8 us -> 3.11 us  [the longest x1 1.56 us: body(): amp = jnp.repeat((residues * -jnp.expm1(-rates)).T, BLOCK, axis=1)]
    unnamed x30 -> x8, local copies, waits for them, and re-layouts: 54.3 us -> 2.8 us
    all_gather x1 -> x0, waiting for transfers between devices: 50.8 us -> none  [prefix(): everything = jax.tree.map(lambda part: lax.all_gather(part, axis), array)]
    another operation x3 -> x0, local copies, waits for them, and re-layouts: 45.6 us -> none  [the longest x2 45.5 us: body(): tiled = jnp.tile(rolled, (1, block))[:, :block * (period - 1)]]
    pallas_call x0 -> x2, Pallas kernels: none -> 39.6 us  [the longest x1 31.5 us: body(): pl.pallas_call(functools.partial(main_kernel, count), out_shape=tuple((pl...]
    select_n x32 -> x0, other arithmetic: 37.4 us -> none  [turn(): return jax.tree.map(lambda a, b: jnp.where(reached, a, b), new, before)]
    dot_general x3 -> x0, matrix products: 27.2 us -> none  [the longest x1 17.1 us: body(): jnp.einsum('gts,gsm->gmt', toeplitz, lanes, precision=lax.Precision.HIGH)]
    slice x7 -> x0, local copies, waits for them, and re-layouts: 26.5 us -> none  [the longest x1 23.1 us: body(): tiled = jnp.tile(rolled, (1, block))[:, :block * (period - 1)]]
  transfers between devices with their start and end apart: 2 -> 0, of which waited for: 1 -> 0; matrix products, arithmetic and copies ran while one was open for 40% -> 0% of each run, Pallas kernels for 0% -> 0%
where the time goes in v1:
time: 47.8 us; the launch traced here: 47.6 us
  Pallas kernels  39.6 us (83%)
  local copies, waits for them, and re-layouts  7.11 us (15%)
  other arithmetic  0.81 us (2%)
    pallas_call x1, Pallas kernels, body(): pl.pallas_call(functools.partial(main_kernel, count), out_shape=tuple((pl...  31.5 us
    pallas_call x1, Pallas kernels, body(): pl.pallas_call(last_kernel, grid=(chunks,), out_shape=jax.ShapeDtypeStruc...  8.16 us
    unnamed x8, local copies, waits for them, and re-layouts  2.8 us
    reshape x1, local copies, waits for them, and re-layouts, body(): amp = jnp.repeat((residues * -jnp.expm1(-rates)).T, BLOCK, axis=1)  1.56 us
    reshape x1, local copies, waits for them, and re-layouts, body(): rate = jnp.repeat(rates.T, BLOCK, axis=1)  1.56 us

profile of v1, /device:TPU:1, one launch (start us, length us, event | category | flops | bytes accessed | tf_op | source)
XLA Modules:
  0.0 47.6 jit_solution(8888439904186047674)
XLA Ops:
  0.0 0.0 copy-start.3
  0.0 0.8 %multiply_bitcast_fusion = f32[16,256]{1,0:T(8,128)S(1)} fusion(f32[256,16]{0,1:T(8,128)} %param.8, f32[256,16]{0,1:T(8,128)} %param.7), kind=kLoop, calls=%fused_computation | loop fusion | flops 12288 | bytes 49152 | tf_op jit(solution)/shard_map/transpose | solution.py:283
  0.8 0.0 copy-start.1
  0.8 0.0 copy-start.2
  0.8 0.6 %broadcast_in_dim.10 = f32[16,256,16]{2,1,0:T(8,128)S(1)} broadcast(f32[16,256]{1,0:T(8,128)S(1)} %multiply_bitcast_fusion), dimensions={0,1} | broadcast | bytes 278528 | tf_op jit(solution)/shard_map/broadcast_in_dim | solution.py:283
  1.4 1.6 %reshape.7.amp = f32[16,4096]{1,0:T(8,128)S(1)} reshape(f32[16,256,16]{2,1,0:T(8,128)S(1)} %broadcast_in_dim.10) | data formatting | bytes 524288 | tf_op jit(solution)/shard_map/reshape | solution.py:283
  3.0 0.0 copy-done.3
  3.0 0.6 %broadcast_in_dim.9 = f32[16,256,16]{2,1,0:T(8,128)S(1)} broadcast(f32[16,256]{1,0:T(8,128)S(1)} %bitcast.5), dimensions={0,1} | broadcast | bytes 278528 | tf_op jit(solution)/shard_map/broadcast_in_dim | solution.py:282
  3.6 1.6 %reshape.6.rate = f32[16,4096]{1,0:T(8,128)S(1)} reshape(f32[16,256,16]{2,1,0:T(8,128)S(1)} %broadcast_in_dim.9) | data formatting | bytes 524288 | tf_op jit(solution)/shard_map/reshape | solution.py:282
  5.2 0.0 copy-done.1
  5.2 0.0 copy-done.2
  5.2 0.0 copy-start
  5.2 2.8 %copy-done = bf16[256,12288]{1,0:T(8,128)(2,1)S(1)} copy-done((bf16[256,12288]{1,0:T(8,128)(2,1)S(1)}, bf16[256,12288]{1,0:T(8,128)(2,1)}, u32[]{:S(2)}) %copy-start) | copy-done | bytes 6291480
  8.0 31.5 %local_part.1 = (f32[256,4096]{1,0:T(8,128)S(1)}, f32[256,4096]{1,0:T(8,128)S(1)}, f32[8,16,4096]{2,1,0:T(8,128)S(1)}, f32[16,4096]{1,0:T(8,128)S(1)}, bf16[32,6...) custom-call(bf16[256,12288]{1,0:T(8,128)(2,1)S(1)} %copy-done, f32[3,12288]{1,0:T(4,128)S(1)} %copy-done.1, ...), custom_call_target="tpu_custom_call" | custom-call | tf_op jit(solution)/shard_map/local_part/pallas_call | solution.py:293
  39.4 8.2 %carried_part.1 = f32[256,4096]{1,0:T(8,128)} custom-call(f32[256,4096]{1,0:T(8,128)S(1)} %get-tuple-element.11.loc, f32[256,4096]{1,0:T(8,128)S(1)} %get-tuple-element.12.query, f32[8,16,4096]{2,1,0:T(8,128)S(1)} %get-tuple-element.13.local_states, f32[16,4096]{1,0:T(8,128)S(1)} %get-tuple-element.14.decay, ...), custom_call_target="tpu_custom_call" | custom-call | tf_op jit(solution)/shard_map/carried_part/pallas_call | solution.py:322
Async XLA Ops:
  0.0 3.0 %copy-start.3 = (f32[256,16]{0,1:T(8,128)S(1)}, f32[256,16]{0,1:T(8,128)}, u32[]{:S(2)}) copy-start(f32[256,16]{0,1:T(8,128)} %param.7) | copy-start | bytes 49156
  0.8 4.3 %copy-start.1 = (f32[3,12288]{1,0:T(4,128)S(1)}, f32[3,12288]{1,0:T(4,128)}, u32[]{:S(2)}) copy-start(f32[3,12288]{1,0:T(4,128)} %taps.1) | copy-start | bytes 442372
  0.8 4.3 %copy-start.2 = (f32[4096]{0:T(1024)S(1)}, f32[4096]{0:T(1024)}, u32[]{:S(2)}) copy-start(f32[4096]{0:T(1024)} %param.9) | copy-start | bytes 49156
  5.2 2.8 %copy-start = (bf16[256,12288]{1,0:T(8,128)(2,1)S(1)}, bf16[256,12288]{1,0:T(8,128)(2,1)}, u32[]{:S(2)}) copy-start(bf16[256,12288]{1,0:T(8,128)(2,1)} %streams.1) | copy-start | bytes 18874372

commit v2 on v1

v2 whole, which is shorter than its diff:
```python
import functools

import jax
import jax.numpy as jnp
from jax import lax
from jax.experimental import pallas as pl
from jax.experimental.pallas import tpu as pltpu
from jax.sharding import PartitionSpec as P

F32 = jnp.float32
BF16 = jnp.bfloat16
LANES = 128
BLOCK = 16
SPAN = 2 * BLOCK
PER_CHUNK = 4
WIDE = PER_CHUNK * LANES
EDGES = 8
UNROLL = 2
MESH = pl.DeviceIdType.MESH


def halves(x):
    high = x.astype(BF16)
    return high, (x - high.astype(F32)).astype(BF16)


def group_mask(lanes):
    row = lax.broadcasted_iota(jnp.int32, (lanes, lanes), 0) // BLOCK
    lane = lax.broadcasted_iota(jnp.int32, (lanes, lanes), 1) // BLOCK
    return row == lane


def spread(mask, x):
    return jnp.where(mask, jnp.concatenate([x] * (mask.shape[0] // BLOCK), axis=0), jnp.zeros((), BF16))


def paired(mask, first, second):
    first, second = halves(first), halves(second)
    left = jnp.concatenate([spread(mask, first[0]), spread(mask, first[1])], axis=0)
    right = jnp.concatenate([spread(mask, second[0]), spread(mask, second[1])], axis=0)
    return jnp.concatenate([left, right], axis=1)


def stack_rows(parts):
    rows = []
    for part, is_low in parts:
        other = jnp.zeros_like(part) if is_low else part
        rows.append(jnp.concatenate([part, other], axis=1))
    return jnp.concatenate(rows, axis=0)


def rim_effect(key_taps, value_taps, edge, rim):
    k0, k1, v0, v1 = edge
    kb, ka, vb, va = rim
    base_k, base_v = key_taps[0] * k0, value_taps[0] * v0
    more_k, more_v = key_taps[1] * ka + key_taps[2] * kb, value_taps[1] * va + value_taps[2] * vb
    first = more_k * base_v + (base_k + more_k) * more_v
    base_k, base_v = key_taps[0] * k1 + key_taps[1] * k0, value_taps[0] * v1 + value_taps[1] * v0
    more_k, more_v = key_taps[2] * ka, value_taps[2] * va
    second = more_k * base_v + (base_k + more_k) * more_v
    return first, second


def main_kernel(
    count, streams, taps_in, rates, residues, skip_in,
    loc, query, forward_high, forward_low, incoming,
    xs, last, taps, skip, few_rates, few_residues, rate, amp, local_states,
    rim_out, rim_in, weights, shifted, sums_out, sums_in, back_out, back_in,
    stream_sem, small_sem, rim_sems, sums_send, sums_recv, back_send, back_recv,
):
    rows, channels = loc.shape
    tiles = channels // LANES
    chunks = tiles // PER_CHUNK
    blocks = rows // BLOCK
    me = lax.axis_index("ctx")

    def stream_copy(s, c):
        return pltpu.make_async_copy(
            streams.at[:, pl.ds(pl.multiple_of(s * channels + c * WIDE, WIDE), WIDE)],
            xs.at[s, c], stream_sem.at[s, c])

    def chunk_at(k):
        return lax.rem(me // PER_CHUNK + 1 + k, chunks)

    small = [pltpu.make_async_copy(a, b, small_sem.at[i]) for i, (a, b) in enumerate((
        (rates, few_rates), (residues, few_residues), (taps_in, taps), (skip_in, skip),
        (streams.at[pl.ds(rows - BLOCK, BLOCK), :], last)))]
    for copy in small:
        copy.start()

    @pl.loop(0, chunks)
    def _(k):
        c = chunk_at(k)
        stream_copy(1, c).start()
        stream_copy(2, c).start()

    barrier = pltpu.get_barrier_semaphore()

    @pl.loop(1, count)
    def _(i):
        pl.semaphore_signal(barrier, inc=1, device_id={"ctx": lax.rem(me + i, count)}, device_id_type=MESH)

    @pl.loop(0, chunks)
    def _(k):
        stream_copy(0, chunk_at(k)).start()

    small[0].wait()
    small[1].wait()
    few = few_rates[...]
    few_residues[...] = few_residues[...] * (few * (1.0 - few / 2 * (1.0 - few / 3 * (1.0 - few / 4 * (
        1.0 - few / 5 * (1.0 - few / 6))))))

    @pl.loop(0, tiles)
    def _(t):
        lane = pl.ds(pl.multiple_of(t * LANES, LANES), LANES)
        inside = lax.broadcasted_iota(jnp.int32, (BLOCK, LANES), 1) % BLOCK
        row = lax.broadcasted_iota(jnp.int32, (BLOCK, LANES), 0)
        group = t * (LANES // BLOCK)
        part = pl.ds(pl.multiple_of(group // LANES * LANES, LANES), LANES)
        pick = lax.broadcasted_iota(jnp.int32, (BLOCK, LANES), 1) // BLOCK + lax.rem(group, LANES)
        r = jnp.take_along_axis(few_rates[:, part], pick, axis=1, mode="promise_in_bounds")
        a = jnp.take_along_axis(few_residues[:, part], pick, axis=1, mode="promise_in_bounds")
        rate[:, lane] = r
        amp[:, lane] = a
        gap = (row - inside).astype(F32)
        near = jnp.zeros((BLOCK, LANES), F32)
        far = jnp.zeros((BLOCK, LANES), F32)
        step = jnp.exp(-float(BLOCK) * r)
        for n in range(BLOCK):
            one = a[n:n + 1] * jnp.exp(-r[n:n + 1] * gap)
            near = near + one
            far = far + one * step[n:n + 1]
        near = halves(jnp.where(row >= inside, near, 0.0))
        far = halves(far)
        back = halves(jnp.exp(-r * (BLOCK - 1.0 - inside.astype(F32))))
        weights[t] = stack_rows([(far[0], False), (far[1], True), (near[0], False), (back[0], False),
                                 (near[1], True), (back[1], True)])

    for copy in small[2:]:
        copy.wait()

    rim_copy = pltpu.make_async_remote_copy(
        src_ref=rim_out, dst_ref=rim_in, send_sem=rim_sems.at[0], recv_sem=rim_sems.at[1],
        device_id={"ctx": lax.rem(me + 1, count)}, device_id_type=MESH)

    def shifted_rows(slot, s, c, j, rim):
        lane = pl.ds(pl.multiple_of(j * LANES, LANES), LANES)
        shifted[slot, pl.ds(6, 2), :] = rim
        for b in range(blocks):
            shifted[slot, pl.ds(8 + BLOCK * b, BLOCK), :] = xs[s, c, pl.ds(BLOCK * b, BLOCK), lane].astype(F32)

    def stream_taps(s, t):
        lane = pl.ds(pl.multiple_of(s * channels + t * LANES, LANES), LANES)
        return [taps[tap:tap + 1, lane] for tap in range(3)]

    def filtered(slot, by, b):
        total = by[0] * shifted[slot, pl.ds(8 + BLOCK * b, BLOCK), :]
        for tap in (1, 2):
            total = total + by[tap] * shifted[slot, pl.ds(8 + BLOCK * b - tap, BLOCK), :]
        return total

    def sums_copy(t):
        return pltpu.make_async_remote_copy(
            src_ref=sums_out.at[t], dst_ref=sums_in.at[me], send_sem=sums_send.at[t], recv_sem=sums_recv.at[me],
            device_id={"ctx": t}, device_id_type=MESH)

    def tile_at(k, i):
        c = chunk_at(k)
        j = lax.rem(me + 1 + i, PER_CHUNK)
        return c, j, c * PER_CHUNK + j

    mask = group_mask(LANES)
    greeted = chunks // 2
    nothing = jnp.zeros((2, LANES), F32)

    def local_tile(u, k, i):
        c, j, t = tile_at(k, i)
        lane = pl.ds(pl.multiple_of(t * LANES, LANES), LANES)
        at_key, at_value = 2 * u, 2 * u + 1
        shifted_rows(at_key, 1, c, j, nothing)
        shifted_rows(at_value, 2, c, j, nothing)
        by_key, by_value = stream_taps(1, t), stream_taps(2, t)
        step = jnp.exp(-float(BLOCK) * rate[:, lane])
        direct = skip[0:1, lane]
        state = jnp.zeros((BLOCK, LANES), F32)
        for quad in range(blocks // 4):
            inner = [filtered(at_key, by_key, 4 * quad + b) * filtered(at_value, by_value, 4 * quad + b)
                     for b in range(4)]
            even = jnp.dot(weights[t], paired(mask, inner[0], inner[2]), preferred_element_type=F32)
            odd = jnp.dot(weights[t, 2 * BLOCK:, :], paired(mask, inner[1], inner[3]), preferred_element_type=F32)
            for b in range(4):
                side = slice((b // 2) * LANES, (b // 2 + 1) * LANES)
                part = odd[:, side] if b % 2 else even[2 * BLOCK:, side]
                value = direct * inner[b] + (part[:BLOCK] + part[2 * BLOCK:3 * BLOCK])
                if b % 2:
                    value = value + (even[:BLOCK, side] + even[BLOCK:2 * BLOCK, side])
                else:
                    local_states[t, (4 * quad + b) // 2] = state
                loc[pl.ds((4 * quad + b) * BLOCK, BLOCK), lane] = value
                state = state * step + (part[BLOCK:2 * BLOCK] + part[3 * BLOCK:])
        sums_out[t, 0:BLOCK] = state
        end = 6 + rows
        sums_out[t, pl.ds(BLOCK, 2)] = shifted[at_key, pl.ds(8, 2), :]
        sums_out[t, pl.ds(BLOCK + 2, 2)] = shifted[at_value, pl.ds(8, 2), :]
        sums_out[t, pl.ds(BLOCK + 4, 2)] = shifted[at_key, pl.ds(end, 2), :]
        sums_out[t, pl.ds(BLOCK + 6, 2)] = shifted[at_value, pl.ds(end, 2), :]

    def local_chunk(k):
        c = chunk_at(k)
        stream_copy(1, c).wait()
        stream_copy(2, c).wait()

        @pl.loop(0, PER_CHUNK, step=UNROLL)
        def _(i):
            for u in range(UNROLL):
                local_tile(u, k, i + u)

    def send_chunk(k):
        for i in range(PER_CHUNK):
            t = tile_at(k, i)[2]

            @pl.when(t != me)
            def _():
                sums_copy(t).start()

    @pl.loop(0, greeted)
    def _(k):
        local_chunk(k)

    @pl.loop(0, 3 * chunks)
    def _(e):
        for p in range(PER_CHUNK):
            lane = pl.ds(pl.multiple_of(e * WIDE + p * LANES, LANES), LANES)
            rim_out[e, 2 * p:2 * p + 2, :] = last[:, lane].astype(F32)[BLOCK - 2:]

    pl.semaphore_wait(barrier, count - 1)
    rim_copy.start()

    @pl.loop(0, greeted)
    def _(k):
        send_chunk(k)

    @pl.loop(greeted, chunks)
    def _(k):
        local_chunk(k)
        send_chunk(k)

    sums_in[me] = sums_out[me]
    rim_copy.wait()
    has_rim = jnp.where(me > 0, 1.0, 0.0)

    def rest_tile(k, j):
        c = chunk_at(k)
        t = c * PER_CHUNK + j
        lane = pl.ds(pl.multiple_of(t * LANES, LANES), LANES)
        r, a = rate[:, lane], amp[:, lane]
        inside = lax.broadcasted_iota(jnp.int32, (BLOCK, LANES), 1) % BLOCK
        row = lax.broadcasted_iota(jnp.int32, (BLOCK, LANES), 0)
        own = row == inside
        r_own = jnp.sum(jnp.where(own, r, 0.0), axis=0, keepdims=True)
        a_own = jnp.sum(jnp.where(own, a, 0.0), axis=0, keepdims=True)
        out = a_own * jnp.exp(-r_own * (row.astype(F32) + 1.0))
        step = jnp.exp(-float(BLOCK) * r_own)
        near = []
        for b in range(blocks):
            high, low = halves(out)
            forward_high[pl.ds(b * BLOCK, BLOCK), lane] = high
            forward_low[pl.ds(b * BLOCK, BLOCK), lane] = low
            if b < 2:
                near.append((high, low))
            out = out * step
        by = stack_rows([(near[0][0], False), (near[1][0], False), (near[0][1], True), (near[1][1], True)])
        rim = [rim_in[s * chunks + c, pl.ds(2 * j, 2), :] * has_rim for s in range(3)]
        edge = sums_out[t, pl.ds(BLOCK, 4)]
        first, second = rim_effect(
            stream_taps(1, t), stream_taps(2, t), [edge[i:i + 1] for i in range(4)],
            [rim[1][0:1], rim[1][1:2], rim[2][0:1], rim[2][1:2]])
        before = jnp.sum(a * jnp.exp(r), axis=0, keepdims=True)
        direct = skip[0:1, lane]
        loc[0:1, lane] += direct * first - before * second
        loc[1:2, lane] += direct * second

        shifted_rows(0, 0, c, j, rim[0])
        by_query = stream_taps(0, t)
        spans = rows // SPAN
        for pair in range(spans // 2):
            both = jnp.dot(by, paired(mask, local_states[t, 2 * pair], local_states[t, 2 * pair + 1]),
                           preferred_element_type=F32)
            for side in range(2):
                value = both[:, side * LANES:(side + 1) * LANES]
                for half in range(2):
                    b = (2 * pair + side) * 2 + half
                    at = pl.ds(b * BLOCK, BLOCK)
                    gate = filtered(0, by_query, b)
                    query[at, lane] = gate
                    loc[at, lane] = gate * (loc[at, lane] + (
                        value[half * BLOCK:(half + 1) * BLOCK] + value[SPAN + half * BLOCK:SPAN + (half + 1) * BLOCK]))

    def rest_chunk(k):
        stream_copy(0, chunk_at(k)).wait()

        @pl.loop(0, PER_CHUNK)
        def _(j):
            rest_tile(k, j)

    answered = chunks // 2

    @pl.loop(0, answered)
    def _(k):
        rest_chunk(k)

    def sums_arrival(d):
        return pltpu.make_async_remote_copy(
            src_ref=sums_out.at[d], dst_ref=sums_in.at[d], send_sem=sums_send.at[d], recv_sem=sums_recv.at[d],
            device_id={"ctx": d}, device_id_type=MESH)

    def back_copy(d):
        return pltpu.make_async_remote_copy(
            src_ref=back_out.at[d], dst_ref=back_in.at[me], send_sem=back_send.at[d], recv_sem=back_recv.at[me],
            device_id={"ctx": d}, device_id_type=MESH)

    def back_arrival(d):
        return pltpu.make_async_remote_copy(
            src_ref=back_out.at[d], dst_ref=back_in.at[d], send_sem=back_send.at[d], recv_sem=back_recv.at[d],
            device_id={"ctx": d}, device_id_type=MESH)

    @pl.loop(1, count)
    def _(i):
        sums_arrival(lax.rem(me + i, count)).wait_recv()

    r = rate[:, pl.ds(pl.multiple_of(me * LANES, LANES), LANES)]
    device_decay = jnp.exp(-float(rows) * r)
    ahead = jnp.exp(r)
    further = ahead * ahead
    key_taps, value_taps = stream_taps(1, me), stream_taps(2, me)
    state = jnp.zeros((BLOCK, LANES), F32)
    for d in range(count):
        if d:
            edge = sums_in[d, BLOCK:BLOCK + EDGES]
            rim = sums_in[d - 1, BLOCK:BLOCK + EDGES]
            first, second = rim_effect(key_taps, value_taps, [edge[i:i + 1] for i in range(4)],
                                       [rim[i:i + 1] for i in range(4, 8)])
            state = state + (ahead * first + further * second)
        back_out[d] = state
        state = state * device_decay + sums_in[d, 0:BLOCK]
    back_in[me] = back_out[me]

    @pl.loop(1, count)
    def _(i):
        back_copy(lax.rem(me + i, count)).start()

    @pl.loop(answered, chunks)
    def _(k):
        rest_chunk(k)

    @pl.loop(1, count)
    def _(i):
        d = lax.rem(me + i, count)
        back_arrival(d).wait_recv()
        sums_arrival(d).wait_send()
        back_copy(d).wait_send()

    for t in range(tiles):
        incoming[:, t * LANES:(t + 1) * LANES] = back_in[t]


def last_kernel(loc, query, forward_high, forward_low, incoming, out):
    step = pl.program_id(0)
    wide = out.shape[1]
    lanes = 2 * LANES
    mask = group_mask(lanes)
    for j in range(wide // lanes):
        lane = pl.ds(pl.multiple_of(step * wide + j * lanes, lanes), lanes)
        high, low = halves(incoming[:, lane])
        high, low = spread(mask, high), spread(mask, low)
        by_high, by_low = forward_high[:, lane], forward_low[:, lane]
        value = jnp.dot(jnp.concatenate([by_high, by_low, by_high], axis=1),
                        jnp.concatenate([high, high, low], axis=0), preferred_element_type=F32)
        out[:, j * lanes:(j + 1) * lanes] = loc[:, lane] + query[:, lane] * value


def body(count, streams, short_filter, rates, residues, skip):
    rows = streams.shape[0]
    channels = skip.shape[0]
    groups = rates.shape[0]
    tiles = channels // LANES
    chunks = tiles // PER_CHUNK
    vmem = pl.BlockSpec(memory_space=pltpu.VMEM)
    hbm = pl.BlockSpec(memory_space=pltpu.HBM)
    shapes = (
        ((rows, channels), F32),
        ((rows, channels), F32),
        ((rows, channels), BF16),
        ((rows, channels), BF16),
        ((BLOCK, channels), F32),
    )
    operands = (streams, short_filter, rates.T, residues.T, skip[None, :])
    operands = [pltpu.with_memory_space_constraint(x, pltpu.HBM) for x in operands]
    parts = pl.pallas_call(
        functools.partial(main_kernel, count),
        out_shape=tuple(pltpu.VMEM(shape, dtype) for shape, dtype in shapes),
        in_specs=[hbm] * 5,
        out_specs=(vmem,) * len(shapes),
        scratch_shapes=[
            pltpu.VMEM((3, chunks, rows, WIDE), BF16),
            pltpu.VMEM((BLOCK, 3 * channels), BF16),
            pltpu.VMEM(short_filter.shape, F32),
            pltpu.VMEM((1, channels), F32),
            pltpu.VMEM((BLOCK, groups), F32),
            pltpu.VMEM((BLOCK, groups), F32),
            pltpu.VMEM((BLOCK, channels), F32),
            pltpu.VMEM((BLOCK, channels), F32),
            pltpu.VMEM((tiles, rows // SPAN, BLOCK, LANES), F32),
            pltpu.VMEM((3 * chunks, 8, LANES), F32),
            pltpu.VMEM((3 * chunks, 8, LANES), F32),
            pltpu.VMEM((tiles, 6 * BLOCK, 2 * LANES), BF16),
            pltpu.VMEM((2 * UNROLL, rows + 8, LANES), F32),
            pltpu.VMEM((count, BLOCK + EDGES, LANES), F32),
            pltpu.VMEM((count, BLOCK + EDGES, LANES), F32),
            pltpu.VMEM((count, BLOCK, LANES), F32),
            pltpu.VMEM((count, BLOCK, LANES), F32),
            pltpu.SemaphoreType.DMA((3, chunks)),
            pltpu.SemaphoreType.DMA((5,)),
            pltpu.SemaphoreType.DMA((2,)),
            pltpu.SemaphoreType.DMA((count,)),
            pltpu.SemaphoreType.DMA((count,)),
            pltpu.SemaphoreType.DMA((count,)),
            pltpu.SemaphoreType.DMA((count,)),
        ],
        compiler_params=pltpu.CompilerParams(
            collective_id=0, has_side_effects=True, vmem_limit_bytes=24 << 20),
        name="local_part",
    )(*operands)
    parts = [pltpu.with_memory_space_constraint(part, pltpu.VMEM) for part in parts]
    return pl.pallas_call(
        last_kernel,
        grid=(chunks,),
        out_shape=jax.ShapeDtypeStruct((rows, channels), F32),
        in_specs=[vmem] * len(parts),
        out_specs=pl.BlockSpec((rows, WIDE), lambda i: (0, i)),
        compiler_params=pltpu.CompilerParams(vmem_limit_bytes=12 << 20),
        name="carried_part",
    )(*parts)


def solution(mesh):
    count = mesh.shape["ctx"]
    in_specs = (P(("dp", "ctx"), None), P(), P(), P(), P())
    out_specs = P(("dp", "ctx"), None)
    return jax.shard_map(functools.partial(body, count), mesh=mesh, in_specs=in_specs, out_specs=out_specs,
                         check_vma=False)
```

time: 47.8 us -> 34 us (0.71)
  local copies, waits for them, and re-layouts: 7.11 us -> 0 us
  Pallas kernels: 39.6 us -> 33.8 us
  other arithmetic: 0.81 us -> 0 us
    reshape x2 -> x0, local copies, waits for them, and re-layouts: 3.11 us -> none  [the longest x1 1.56 us: body(): amp = jnp.repeat((residues * -jnp.expm1(-rates)).T, BLOCK, axis=1)]
    pallas_call x1, Pallas kernels: 8.16 us -> 5.15 us  [body(): pl.pallas_call(last_kernel, grid=(chunks,), out_shape=jax.ShapeDtypeStruc...]
    unnamed x8 -> x0, local copies, waits for them, and re-layouts: 2.8 us -> none
    pallas_call x1, Pallas kernels: 31.5 us -> 28.7 us  [body(): pl.pallas_call(functools.partial(main_kernel, count), out_shape=tuple((pl...]
    broadcast_in_dim x2 -> x0, local copies, waits for them, and re-layouts: 1.2 us -> none  [the longest x1 0.6 us: body(): rate = jnp.repeat(rates.T, BLOCK, axis=1)]
    transpose x1 -> x0, other arithmetic: 0.81 us -> none  [body(): amp = jnp.repeat((residues * -jnp.expm1(-rates)).T, BLOCK, axis=1)]
where the time goes in v2:
time: 34 us; the launch traced here: 33.8 us
  Pallas kernels  33.8 us (99%)
    pallas_call x1, Pallas kernels, body(): pl.pallas_call(functools.partial(main_kernel, count), out_shape=tuple((pl...  28.7 us
    pallas_call x1, Pallas kernels, body(): pl.pallas_call(last_kernel, grid=(chunks,), out_shape=jax.ShapeDtypeStruc...  5.15 us

profile of v2, /device:TPU:1, one launch (start us, length us, event | category | flops | bytes accessed | tf_op | source)
XLA Modules:
  0.0 33.8 jit_solution(14707997498338368464)
XLA Ops:
  0.0 28.7 %local_part.1 = (f32[256,4096]{1,0:T(8,128)S(1)}, f32[256,4096]{1,0:T(8,128)S(1)}, bf16[256,4096]{1,0:T(8,128)(2,1)S(1)}, bf16[256,4096]{1,0:T(8,128)(2,1)S(1)}, f32[16,4096]{1,0:T(8,128)S(1)}) custom-call(bf16[256,12288]{1,0:T(8,128)(2,1)} %streams.1, f32[3,12288]{1,0:T(4,128)} %taps_in.1, f32[16,256]{1,0:T(8,128)} %bitcast.3, f32[16,256]{1,0:T(8,128)} %bitcast.4, ...), custom_call_target="tpu_custom_call" | custom-call | tf_op jit(solution)/shard_map/local_part/pallas_call | solution.py:399
  28.7 5.2 %carried_part.1 = f32[256,4096]{1,0:T(8,128)} custom-call(f32[256,4096]{1,0:T(8,128)S(1)} %get-tuple-element.10.loc, f32[256,4096]{1,0:T(8,128)S(1)} %get-tuple-element.11.query, bf16[256,4096]{1,0:T(8,128)(2,1)S(1)} %get-tuple-element.12.forward_high, bf16[256,4096]{1,0:T(8,128)(2,1)S(1)} %get-tuple-element.13.forward_low, ...), custom_call_target="tpu_custom_call" | custom-call | tf_op jit(solution)/shard_map/carried_part/pallas_call | solution.py:435

commit v3 on v2

v3 whole, which is shorter than its diff:
```python
import functools

import jax
import jax.numpy as jnp
from jax import lax
from jax.experimental import pallas as pl
from jax.experimental.pallas import tpu as pltpu
from jax.sharding import PartitionSpec as P

F32 = jnp.float32
BF16 = jnp.bfloat16
LANES = 128
BLOCK = 16
SPAN = 2 * BLOCK
PER_CHUNK = 4
WIDE = PER_CHUNK * LANES
EDGES = 8
PAIR = 2 * LANES
UNROLL = 2
MESH = pl.DeviceIdType.MESH


def halves(x):
    high = x.astype(BF16)
    return high, (x - high.astype(F32)).astype(BF16)


def group_mask(lanes):
    row = lax.broadcasted_iota(jnp.int32, (lanes, lanes), 0) // BLOCK
    lane = lax.broadcasted_iota(jnp.int32, (lanes, lanes), 1) // BLOCK
    return row == lane


def spread(mask, x):
    return jnp.where(mask, jnp.concatenate([x] * (mask.shape[0] // BLOCK), axis=0), jnp.zeros((), BF16))


def paired(mask, first, second):
    left = jnp.concatenate([spread(mask, first[0]), spread(mask, first[1])], axis=0)
    right = jnp.concatenate([spread(mask, second[0]), spread(mask, second[1])], axis=0)
    return jnp.concatenate([left, right], axis=1)


def stack_rows(parts):
    rows = []
    for part, is_low in parts:
        other = jnp.zeros_like(part) if is_low else part
        rows.append(jnp.concatenate([part, other], axis=1))
    return jnp.concatenate(rows, axis=0)


def rim_effect(key_taps, value_taps, edge, rim):
    k0, k1, v0, v1 = edge
    kb, ka, vb, va = rim
    base_k, base_v = key_taps[0] * k0, value_taps[0] * v0
    more_k, more_v = key_taps[1] * ka + key_taps[2] * kb, value_taps[1] * va + value_taps[2] * vb
    first = more_k * base_v + (base_k + more_k) * more_v
    base_k, base_v = key_taps[0] * k1 + key_taps[1] * k0, value_taps[0] * v1 + value_taps[1] * v0
    more_k, more_v = key_taps[2] * ka, value_taps[2] * va
    second = more_k * base_v + (base_k + more_k) * more_v
    return first, second


def main_kernel(
    count, streams, taps_in, rates, residues, skip_in,
    loc, query, forward_high, forward_low, incoming,
    xs, last, taps, skip, few_rates, few_amps, backward, u_high, u_low, first_rows,
    rim_out, rim_in, shifted, sums_out, sums_in, back_out, back_in,
    stream_sem, small_sem, rim_sems, sums_send, sums_recv, back_send, back_recv,
):
    rows, channels = loc.shape
    tiles = channels // LANES
    chunks = tiles // PER_CHUNK
    blocks = rows // BLOCK
    me = lax.axis_index("ctx")

    def stream_copy(s, c):
        return pltpu.make_async_copy(
            streams.at[:, pl.ds(pl.multiple_of(s * channels + c * WIDE, WIDE), WIDE)],
            xs.at[s, c], stream_sem.at[s, c])

    def chunk_at(k):
        return lax.rem(me // PER_CHUNK + 1 + k, chunks)

    small = [pltpu.make_async_copy(a, b, small_sem.at[i]) for i, (a, b) in enumerate((
        (rates, few_rates), (residues, few_amps), (taps_in, taps), (skip_in, skip),
        (streams.at[pl.ds(rows - BLOCK, BLOCK), :], last)))]
    for copy in small:
        copy.start()

    @pl.loop(0, chunks)
    def _(k):
        c = chunk_at(k)
        stream_copy(1, c).start()
        stream_copy(2, c).start()

    barrier = pltpu.get_barrier_semaphore()

    @pl.loop(1, count)
    def _(i):
        pl.semaphore_signal(barrier, inc=1, device_id={"ctx": lax.rem(me + i, count)}, device_id_type=MESH)

    @pl.loop(0, chunks)
    def _(k):
        stream_copy(0, chunk_at(k)).start()

    small[0].wait()
    small[1].wait()
    few = few_rates[...]
    few_amps[...] = few_amps[...] * (few * (1.0 - few / 2 * (1.0 - few / 3 * (1.0 - few / 4 * (
        1.0 - few / 5 * (1.0 - few / 6))))))

    def picked(ref, group, index):
        part = pl.ds(pl.multiple_of(group // LANES * LANES, LANES), LANES)
        return jnp.take_along_axis(ref[:, part], index + lax.rem(group, LANES), axis=1, mode="promise_in_bounds")

    @pl.loop(0, tiles // 2)
    def _(t):
        zero = jnp.zeros((BLOCK, LANES), jnp.int32)
        gap = LANES - 1.0 - lax.broadcasted_iota(jnp.int32, (BLOCK, LANES), 1).astype(F32)
        for g in range(PAIR // BLOCK):
            r = picked(few_rates, t * (PAIR // BLOCK) + g, zero)
            piece = jnp.exp(-r * gap)
            step = jnp.exp(-float(LANES) * r)
            pieces = [piece]
            for _ in range(rows // LANES - 1):
                pieces.append(pieces[-1] * step)
            for i, piece in enumerate(pieces[::-1]):
                high, low = halves(piece)
                backward[t, pl.ds(g * BLOCK, BLOCK), i * LANES:(i + 1) * LANES] = high
                backward[t, pl.ds(g * BLOCK, BLOCK), rows + i * LANES:rows + (i + 1) * LANES] = low

    for copy in small[2:]:
        copy.wait()

    rim_copy = pltpu.make_async_remote_copy(
        src_ref=rim_out, dst_ref=rim_in, send_sem=rim_sems.at[0], recv_sem=rim_sems.at[1],
        device_id={"ctx": lax.rem(me + 1, count)}, device_id_type=MESH)

    def shifted_rows(slot, s, c, j):
        lane = pl.ds(pl.multiple_of(j * LANES, LANES), LANES)
        shifted[slot, pl.ds(6, 2), :] = jnp.zeros((2, LANES), F32)
        for b in range(blocks):
            shifted[slot, pl.ds(8 + BLOCK * b, BLOCK), :] = xs[s, c, pl.ds(BLOCK * b, BLOCK), lane].astype(F32)

    def stream_taps(s, t):
        lane = pl.ds(pl.multiple_of(s * channels + t * LANES, LANES), LANES)
        return [taps[tap:tap + 1, lane] for tap in range(3)]

    def filtered(slot, by, b):
        total = by[0] * shifted[slot, pl.ds(8 + BLOCK * b, BLOCK), :]
        for tap in (1, 2):
            total = total + by[tap] * shifted[slot, pl.ds(8 + BLOCK * b - tap, BLOCK), :]
        return total

    def sums_copy(t):
        return pltpu.make_async_remote_copy(
            src_ref=sums_out.at[t], dst_ref=sums_in.at[me], send_sem=sums_send.at[t], recv_sem=sums_recv.at[me],
            device_id={"ctx": t}, device_id_type=MESH)

    def pair_at(k, i):
        return chunk_at(k), lax.rem(me // 2 + i, PER_CHUNK // 2)

    mask = group_mask(LANES)

    def sums_pair(k, i):
        c, p = pair_at(k, i)
        sides = []
        for side in range(2):
            j = 2 * p + side
            t = c * PER_CHUNK + j
            lane = pl.ds(pl.multiple_of(t * LANES, LANES), LANES)
            at_key, at_value = 2 * side, 2 * side + 1
            shifted_rows(at_key, 1, c, j)
            shifted_rows(at_value, 2, c, j)
            by_key, by_value = stream_taps(1, t), stream_taps(2, t)
            direct = skip[0:1, lane]
            highs, lows = [], []
            for b in range(blocks):
                at = pl.ds(b * BLOCK, BLOCK)
                inner = filtered(at_key, by_key, b) * filtered(at_value, by_value, b)
                loc[at, lane] = direct * inner
                high, low = halves(inner)
                u_high[at, lane] = high
                u_low[at, lane] = low
                highs.append(high)
                lows.append(low)
            sides.append((jnp.concatenate(highs, axis=0), jnp.concatenate(lows, axis=0)))
            end = 6 + rows
            sums_out[t, pl.ds(BLOCK, 2)] = shifted[at_key, pl.ds(8, 2), :]
            sums_out[t, pl.ds(BLOCK + 2, 2)] = shifted[at_value, pl.ds(8, 2), :]
            sums_out[t, pl.ds(BLOCK + 4, 2)] = shifted[at_key, pl.ds(end, 2), :]
            sums_out[t, pl.ds(BLOCK + 6, 2)] = shifted[at_value, pl.ds(end, 2), :]
        pair = c * (PER_CHUNK // 2) + p
        high, low = [jnp.concatenate([sides[0][i], sides[1][i]], axis=1) for i in range(2)]
        by = backward[pair]
        every = jnp.dot(jnp.concatenate([by, by[:, :rows]], axis=1), jnp.concatenate([high, high, low], axis=0),
                        preferred_element_type=F32)
        own = lax.broadcasted_iota(jnp.int32, (BLOCK, LANES), 1) // BLOCK
        for side in range(2):
            total = jnp.zeros((BLOCK, LANES), F32)
            for g in range(LANES // BLOCK):
                at = (side * (LANES // BLOCK) + g) * BLOCK
                total = jnp.where(own == g, every[at:at + BLOCK, side * LANES:(side + 1) * LANES], total)
            sums_out[c * PER_CHUNK + 2 * p + side, 0:BLOCK] = total

    def sums_chunk(k):
        c = chunk_at(k)
        stream_copy(1, c).wait()
        stream_copy(2, c).wait()

        @pl.loop(0, PER_CHUNK // 2)
        def _(i):
            sums_pair(k, i)

    def send_chunk(k):
        for i in range(PER_CHUNK // 2):
            c, p = pair_at(k, i)
            for side in range(2):
                t = c * PER_CHUNK + 2 * p + side

                @pl.when(t != me)
                def _():
                    sums_copy(t).start()

    greeted = chunks // 2

    @pl.loop(0, greeted)
    def _(k):
        sums_chunk(k)

    pl.semaphore_wait(barrier, count - 1)

    @pl.loop(0, greeted)
    def _(k):
        send_chunk(k)

    @pl.loop(greeted, chunks)
    def _(k):
        sums_chunk(k)
        send_chunk(k)

    sums_in[me] = sums_out[me]

    @pl.loop(0, 3 * chunks)
    def _(e):
        for p in range(PER_CHUNK):
            lane = pl.ds(pl.multiple_of(e * WIDE + p * LANES, LANES), LANES)
            rim_out[e, 2 * p:2 * p + 2, :] = last[:, lane].astype(F32)[BLOCK - 2:]

    rim_copy.start()

    @pl.loop(0, chunks)
    def _(k):
        stream_copy(0, chunk_at(k)).wait()

    def rest_tile(u, t):
        lane = pl.ds(pl.multiple_of(t * LANES, LANES), LANES)
        inside = lax.broadcasted_iota(jnp.int32, (BLOCK, LANES), 1) % BLOCK
        row = lax.broadcasted_iota(jnp.int32, (BLOCK, LANES), 0)
        pick = lax.broadcasted_iota(jnp.int32, (BLOCK, LANES), 1) // BLOCK
        group = t * (LANES // BLOCK)
        r, a = picked(few_rates, group, pick), picked(few_amps, group, pick)
        own = row == inside
        r_own = jnp.sum(jnp.where(own, r, 0.0), axis=0, keepdims=True)
        a_own = jnp.sum(jnp.where(own, a, 0.0), axis=0, keepdims=True)
        out = a_own * jnp.exp(-r_own * (row.astype(F32) + 1.0))
        step = jnp.exp(-float(BLOCK) * r_own)
        near = []
        for b in range(blocks):
            high, low = halves(out)
            forward_high[pl.ds(b * BLOCK, BLOCK), lane] = high
            forward_low[pl.ds(b * BLOCK, BLOCK), lane] = low
            if b < 2:
                near.append((high, low))
            out = out * step
        by = stack_rows([(near[0][0], False), (near[1][0], False), (near[0][1], True), (near[1][1], True)])
        inside = inside.astype(F32)
        high, low = halves(jnp.exp(r * (inside + 1.0)))
        span = jnp.dot(by, jnp.concatenate([spread(mask, high), spread(mask, low)], axis=0), preferred_element_type=F32)
        span = span[:SPAN] + span[SPAN:]
        near = halves(jnp.where(row.astype(F32) >= inside, span[:BLOCK], 0.0))
        far = halves(span[BLOCK:])
        back = halves(jnp.exp(-r * (BLOCK - 1.0 - inside)))
        weights = stack_rows([(far[0], False), (far[1], True), (near[0], False), (back[0], False),
                              (near[1], True), (back[1], True)])
        shifted_rows(u, 0, t // PER_CHUNK, lax.rem(t, PER_CHUNK))
        by_query = stream_taps(0, t)
        step = jnp.exp(-float(BLOCK) * r)
        state = jnp.zeros((BLOCK, LANES), F32)

        def block_u(b):
            at = pl.ds(b * BLOCK, BLOCK)
            return u_high[at, lane], u_low[at, lane]

        for quad in range(blocks // 4):
            even = jnp.dot(weights, paired(mask, block_u(4 * quad), block_u(4 * quad + 2)), preferred_element_type=F32)
            odd = jnp.dot(weights[2 * BLOCK:], paired(mask, block_u(4 * quad + 1), block_u(4 * quad + 3)),
                          preferred_element_type=F32)
            states, values = [], []
            for b in range(4):
                side = slice((b // 2) * LANES, (b // 2 + 1) * LANES)
                part = odd[:, side] if b % 2 else even[2 * BLOCK:, side]
                value = loc[pl.ds((4 * quad + b) * BLOCK, BLOCK), lane] + (part[:BLOCK] + part[2 * BLOCK:3 * BLOCK])
                if b % 2:
                    value = value + (even[:BLOCK, side] + even[BLOCK:2 * BLOCK, side])
                else:
                    states.append(halves(state))
                values.append(value)
                state = state * step + (part[BLOCK:2 * BLOCK] + part[3 * BLOCK:])
            both = jnp.dot(by, paired(mask, *states), preferred_element_type=F32)
            for b in range(4):
                value = both[:, (b // 2) * LANES:(b // 2 + 1) * LANES]
                half = (b % 2) * BLOCK
                total = values[b] + (value[half:half + BLOCK] + value[SPAN + half:SPAN + half + BLOCK])
                if quad == 0 and b == 0:
                    first_rows[t] = total[:8]
                at = pl.ds((4 * quad + b) * BLOCK, BLOCK)
                gate = filtered(u, by_query, 4 * quad + b)
                query[at, lane] = gate
                loc[at, lane] = gate * total

    answered = tiles // 2

    @pl.loop(0, answered, step=UNROLL)
    def _(t):
        for u in range(UNROLL):
            rest_tile(u, t + u)

    def sums_arrival(d):
        return pltpu.make_async_remote_copy(
            src_ref=sums_out.at[d], dst_ref=sums_in.at[d], send_sem=sums_send.at[d], recv_sem=sums_recv.at[d],
            device_id={"ctx": d}, device_id_type=MESH)

    def back_copy(d):
        return pltpu.make_async_remote_copy(
            src_ref=back_out.at[d], dst_ref=back_in.at[me], send_sem=back_send.at[d], recv_sem=back_recv.at[me],
            device_id={"ctx": d}, device_id_type=MESH)

    def back_arrival(d):
        return pltpu.make_async_remote_copy(
            src_ref=back_out.at[d], dst_ref=back_in.at[d], send_sem=back_send.at[d], recv_sem=back_recv.at[d],
            device_id={"ctx": d}, device_id_type=MESH)

    @pl.loop(1, count)
    def _(i):
        sums_arrival(lax.rem(me + i, count)).wait_recv()

    pick = lax.broadcasted_iota(jnp.int32, (BLOCK, LANES), 1) // BLOCK
    r = picked(few_rates, me * (LANES // BLOCK), pick)
    device_decay = jnp.exp(-float(rows) * r)
    ahead = jnp.exp(r)
    further = ahead * ahead
    key_taps, value_taps = stream_taps(1, me), stream_taps(2, me)
    state = jnp.zeros((BLOCK, LANES), F32)
    for d in range(count):
        if d:
            edge = sums_in[d, BLOCK:BLOCK + EDGES]
            rim = sums_in[d - 1, BLOCK:BLOCK + EDGES]
            first, second = rim_effect(key_taps, value_taps, [edge[i:i + 1] for i in range(4)],
                                       [rim[i:i + 1] for i in range(4, 8)])
            state = state + (ahead * first + further * second)
        back_out[d] = state
        state = state * device_decay + sums_in[d, 0:BLOCK]
    back_in[me] = back_out[me]

    @pl.loop(1, count)
    def _(i):
        back_copy(lax.rem(me + i, count)).start()

    @pl.loop(answered, tiles, step=UNROLL)
    def _(t):
        for u in range(UNROLL):
            rest_tile(u, t + u)

    rim_copy.wait()
    has_rim = jnp.where(me > 0, 1.0, 0.0)

    @pl.loop(0, chunks)
    def _(c):
        for j in range(PER_CHUNK):
            t = c * PER_CHUNK + j
            lane = pl.ds(pl.multiple_of(t * LANES, LANES), LANES)
            rim = [rim_in[s * chunks + c, 2 * j:2 * j + 2, :] * has_rim for s in range(3)]
            edge = sums_out[t, pl.ds(BLOCK, 4)]
            first, second = rim_effect(
                stream_taps(1, t), stream_taps(2, t), [edge[i:i + 1] for i in range(4)],
                [rim[1][0:1], rim[1][1:2], rim[2][0:1], rim[2][1:2]])
            r, a = picked(few_rates, t * (LANES // BLOCK), pick), picked(few_amps, t * (LANES // BLOCK), pick)
            before = jnp.sum(a * jnp.exp(r), axis=0, keepdims=True)
            direct = skip[0:1, lane]
            by_query = stream_taps(0, t)
            total = first_rows[t]
            gate = query[0:8, lane]
            gates = (gate[0:1] + by_query[1] * rim[0][1:2] + by_query[2] * rim[0][0:1],
                     gate[1:2] + by_query[2] * rim[0][1:2])
            totals = (total[0:1] + direct * first - before * second, total[1:2] + direct * second)
            for i in range(2):
                query[i:i + 1, lane] = gates[i]
                loc[i:i + 1, lane] = gates[i] * totals[i]

    @pl.loop(1, count)
    def _(i):
        d = lax.rem(me + i, count)
        back_arrival(d).wait_recv()
        sums_arrival(d).wait_send()
        back_copy(d).wait_send()

    for t in range(tiles):
        incoming[:, t * LANES:(t + 1) * LANES] = back_in[t]


def last_kernel(loc, query, forward_high, forward_low, incoming, out, held, sems):
    channels = loc.shape[1]
    mask = group_mask(PAIR)
    copies = []
    for start in range(0, channels, WIDE):
        for first in range(start, start + WIDE, PAIR):
            lane = slice(first, first + PAIR)
            high, low = halves(incoming[:, lane])
            high, low = spread(mask, high), spread(mask, low)
            by_high, by_low = forward_high[:, lane], forward_low[:, lane]
            value = jnp.dot(jnp.concatenate([by_high, by_low, by_high], axis=1),
                            jnp.concatenate([high, high, low], axis=0), preferred_element_type=F32)
            held[:, lane] = loc[:, lane] + query[:, lane] * value
        lane = slice(start, start + WIDE)
        copies.append(pltpu.make_async_copy(held.at[:, lane], out.at[:, lane], sems.at[start // WIDE]))
        copies[-1].start()
    for copy in copies:
        copy.wait()


def body(count, streams, short_filter, rates, residues, skip):
    rows = streams.shape[0]
    channels = skip.shape[0]
    groups = rates.shape[0]
    tiles = channels // LANES
    chunks = tiles // PER_CHUNK
    vmem = pl.BlockSpec(memory_space=pltpu.VMEM)
    hbm = pl.BlockSpec(memory_space=pltpu.HBM)
    shapes = (
        ((rows, channels), F32),
        ((rows, channels), F32),
        ((rows, channels), BF16),
        ((rows, channels), BF16),
        ((BLOCK, channels), F32),
    )
    operands = (streams, short_filter, rates.T, residues.T, skip[None, :])
    operands = [pltpu.with_memory_space_constraint(x, pltpu.HBM) for x in operands]
    parts = pl.pallas_call(
        functools.partial(main_kernel, count),
        out_shape=tuple(pltpu.VMEM(shape, dtype) for shape, dtype in shapes),
        in_specs=[hbm] * 5,
        out_specs=(vmem,) * len(shapes),
        scratch_shapes=[
            pltpu.VMEM((3, chunks, rows, WIDE), BF16),
            pltpu.VMEM((BLOCK, 3 * channels), BF16),
            pltpu.VMEM(short_filter.shape, F32),
            pltpu.VMEM((1, channels), F32),
            pltpu.VMEM((BLOCK, groups), F32),
            pltpu.VMEM((BLOCK, groups), F32),
            pltpu.VMEM((tiles // 2, PAIR, 2 * rows), BF16),
            pltpu.VMEM((rows, channels), BF16),
            pltpu.VMEM((rows, channels), BF16),
            pltpu.VMEM((tiles, 8, LANES), F32),
            pltpu.VMEM((3 * chunks, 8, LANES), F32),
            pltpu.VMEM((3 * chunks, 8, LANES), F32),
            pltpu.VMEM((4, rows + 8, LANES), F32),
            pltpu.VMEM((count, BLOCK + EDGES, LANES), F32),
            pltpu.VMEM((count, BLOCK + EDGES, LANES), F32),
            pltpu.VMEM((count, BLOCK, LANES), F32),
            pltpu.VMEM((count, BLOCK, LANES), F32),
            pltpu.SemaphoreType.DMA((3, chunks)),
            pltpu.SemaphoreType.DMA((5,)),
            pltpu.SemaphoreType.DMA((2,)),
            pltpu.SemaphoreType.DMA((count,)),
            pltpu.SemaphoreType.DMA((count,)),
            pltpu.SemaphoreType.DMA((count,)),
            pltpu.SemaphoreType.DMA((count,)),
        ],
        compiler_params=pltpu.CompilerParams(
            collective_id=0, has_side_effects=True, vmem_limit_bytes=24 << 20),
        name="local_part",
    )(*operands)
    parts = [pltpu.with_memory_space_constraint(part, pltpu.VMEM) for part in parts]
    return pl.pallas_call(
        last_kernel,
        out_shape=jax.ShapeDtypeStruct((rows, channels), F32),
        in_specs=[vmem] * len(parts),
        out_specs=hbm,
        scratch_shapes=[pltpu.VMEM((rows, channels), F32), pltpu.SemaphoreType.DMA((chunks,))],
        compiler_params=pltpu.CompilerParams(vmem_limit_bytes=16 << 20),
        name="carried_part",
    )(*parts)


def solution(mesh):
    count = mesh.shape["ctx"]
    in_specs = (P(("dp", "ctx"), None), P(), P(), P(), P())
    out_specs = P(("dp", "ctx"), None)
    return jax.shard_map(functools.partial(body, count), mesh=mesh, in_specs=in_specs, out_specs=out_specs,
                         check_vma=False)
```

time: 34 us -> 42 us (1.24)
  Pallas kernels: 33.8 us -> 41.9 us
    pallas_call x1, Pallas kernels: 28.7 us -> 39.2 us  [body(): pl.pallas_call(functools.partial(main_kernel, count), out_shape=tuple((pl...]
    pallas_call x1, Pallas kernels: 5.15 us -> 2.68 us  [body(): pl.pallas_call(last_kernel, out_shape=jax.ShapeDtypeStruct((rows, channel...]
where the time goes in v3:
time: 42 us; the launch traced here: 41.9 us
  Pallas kernels  41.9 us (100%)
    pallas_call x1, Pallas kernels, body(): pl.pallas_call(functools.partial(main_kernel, count), out_shape=tuple((pl...  39.2 us
    pallas_call x1, Pallas kernels, body(): pl.pallas_call(last_kernel, out_shape=jax.ShapeDtypeStruct((rows, channel...  2.68 us

profile of v3, /device:TPU:1, one launch (start us, length us, event | category | flops | bytes accessed | tf_op | source)
XLA Modules:
  0.0 41.9 jit_solution(7192622037278279992)
XLA Ops:
  0.0 39.2 %local_part.1 = (f32[256,4096]{1,0:T(8,128)S(1)}, f32[256,4096]{1,0:T(8,128)S(1)}, bf16[256,4096]{1,0:T(8,128)(2,1)S(1)}, bf16[256,4096]{1,0:T(8,128)(2,1)S(1)}, f32[16,4096]{1,0:T(8,128)S(1)}) custom-call(bf16[256,12288]{1,0:T(8,128)(2,1)} %streams.1, f32[3,12288]{1,0:T(4,128)} %taps_in.1, f32[16,256]{1,0:T(8,128)} %bitcast.3, f32[16,256]{1,0:T(8,128)} %bitcast.4, ...), custom_call_target="tpu_custom_call" | custom-call | tf_op jit(solution)/shard_map/local_part/pallas_call | solution.py:450
  39.2 2.7 %carried_part.1 = f32[256,4096]{1,0:T(8,128)} custom-call(f32[256,4096]{1,0:T(8,128)S(1)} %get-tuple-element.10.loc, f32[256,4096]{1,0:T(8,128)S(1)} %get-tuple-element.11.query, bf16[256,4096]{1,0:T(8,128)(2,1)S(1)} %get-tuple-element.12.forward_high, bf16[256,4096]{1,0:T(8,128)(2,1)S(1)} %get-tuple-element.13.forward_low, ...), custom_call_target="tpu_custom_call" | custom-call | tf_op jit(solution)/shard_map/carried_part/pallas_call | solution.py:486

commit v4 on v3

--- a/solution.py
+++ b/solution.py
@@ -16,7 +16,7 @@
 WIDE = PER_CHUNK * LANES
 EDGES = 8
 PAIR = 2 * LANES
-UNROLL = 2
+UNROLL = 4
 MESH = pl.DeviceIdType.MESH
 
 
@@ -65,7 +65,7 @@
     count, streams, taps_in, rates, residues, skip_in,
     loc, query, forward_high, forward_low, incoming,
     xs, last, taps, skip, few_rates, few_amps, backward, u_high, u_low, first_rows,
-    rim_out, rim_in, shifted, sums_out, sums_in, back_out, back_in,
+    weights, states, rim_out, rim_in, shifted, sums_out, sums_in, back_out, back_in,
     stream_sem, small_sem, rim_sems, sums_send, sums_recv, back_send, back_recv,
 ):
     rows, channels = loc.shape
@@ -158,14 +158,15 @@
             src_ref=sums_out.at[t], dst_ref=sums_in.at[me], send_sem=sums_send.at[t], recv_sem=sums_recv.at[me],
             device_id={"ctx": t}, device_id_type=MESH)
 
-    def pair_at(k, i):
-        return chunk_at(k), lax.rem(me // 2 + i, PER_CHUNK // 2)
+    halfs = PER_CHUNK // 2
+
+    def pair_at(q):
+        return chunk_at(q // halfs), lax.rem(me // 2 + lax.rem(q, halfs), halfs)
 
     mask = group_mask(LANES)
 
-    def sums_pair(k, i):
-        c, p = pair_at(k, i)
-        sides = []
+    def values_pair(q):
+        c, p = pair_at(q)
         for side in range(2):
             j = 2 * p + side
             t = c * PER_CHUNK + j
@@ -175,24 +176,22 @@
             shifted_rows(at_value, 2, c, j)
             by_key, by_value = stream_taps(1, t), stream_taps(2, t)
             direct = skip[0:1, lane]
-            highs, lows = [], []
             for b in range(blocks):
                 at = pl.ds(b * BLOCK, BLOCK)
                 inner = filtered(at_key, by_key, b) * filtered(at_value, by_value, b)
                 loc[at, lane] = direct * inner
-                high, low = halves(inner)
-                u_high[at, lane] = high
-                u_low[at, lane] = low
-                highs.append(high)
-                lows.append(low)
-            sides.append((jnp.concatenate(highs, axis=0), jnp.concatenate(lows, axis=0)))
+                u_high[at, lane], u_low[at, lane] = halves(inner)
             end = 6 + rows
             sums_out[t, pl.ds(BLOCK, 2)] = shifted[at_key, pl.ds(8, 2), :]
             sums_out[t, pl.ds(BLOCK + 2, 2)] = shifted[at_value, pl.ds(8, 2), :]
             sums_out[t, pl.ds(BLOCK + 4, 2)] = shifted[at_key, pl.ds(end, 2), :]
             sums_out[t, pl.ds(BLOCK + 6, 2)] = shifted[at_value, pl.ds(end, 2), :]
-        pair = c * (PER_CHUNK // 2) + p
-        high, low = [jnp.concatenate([sides[0][i], sides[1][i]], axis=1) for i in range(2)]
+
+    def sums_pair(q):
+        c, p = pair_at(q)
+        pair = c * halfs + p
+        lane = pl.ds(pl.multiple_of(pair * PAIR, PAIR), PAIR)
+        high, low = u_high[:, lane], u_low[:, lane]
         by = backward[pair]
         every = jnp.dot(jnp.concatenate([by, by[:, :rows]], axis=1), jnp.concatenate([high, high, low], axis=0),
                         preferred_element_type=F32)
@@ -202,44 +201,50 @@
             for g in range(LANES // BLOCK):
                 at = (side * (LANES // BLOCK) + g) * BLOCK
                 total = jnp.where(own == g, every[at:at + BLOCK, side * LANES:(side + 1) * LANES], total)
-            sums_out[c * PER_CHUNK + 2 * p + side, 0:BLOCK] = total
-
-    def sums_chunk(k):
-        c = chunk_at(k)
-        stream_copy(1, c).wait()
-        stream_copy(2, c).wait()
-
-        @pl.loop(0, PER_CHUNK // 2)
-        def _(i):
-            sums_pair(k, i)
-
-    def send_chunk(k):
-        for i in range(PER_CHUNK // 2):
-            c, p = pair_at(k, i)
-            for side in range(2):
-                t = c * PER_CHUNK + 2 * p + side
-
-                @pl.when(t != me)
-                def _():
-                    sums_copy(t).start()
-
-    greeted = chunks // 2
-
-    @pl.loop(0, greeted)
-    def _(k):
-        sums_chunk(k)
+            sums_out[2 * pair + side, 0:BLOCK] = total
+
+    def send_pair(q):
+        c, p = pair_at(q)
+        for side in range(2):
+            t = c * PER_CHUNK + 2 * p + side
+
+            @pl.when(t != me)
+            def _():
+                sums_copy(t).start()
+
+    def chunk_wait(q):
+        @pl.when(lax.rem(q, halfs) == 0)
+        def _():
+            c = chunk_at(q // halfs)
+            stream_copy(1, c).wait()
+            stream_copy(2, c).wait()
+
+    pairs = tiles // 2
+    greeted = pairs // 2
+    chunk_wait(0)
+    values_pair(0)
+
+    @pl.loop(1, greeted)
+    def _(q):
+        chunk_wait(q)
+        sums_pair(q - 1)
+        values_pair(q)
 
     pl.semaphore_wait(barrier, count - 1)
 
-    @pl.loop(0, greeted)
-    def _(k):
-        send_chunk(k)
-
-    @pl.loop(greeted, chunks)
-    def _(k):
-        sums_chunk(k)
-        send_chunk(k)
-
+    @pl.loop(0, greeted - 1)
+    def _(q):
+        send_pair(q)
+
+    @pl.loop(greeted, pairs)
+    def _(q):
+        chunk_wait(q)
+        sums_pair(q - 1)
+        values_pair(q)
+        send_pair(q - 1)
+
+    sums_pair(pairs - 1)
+    send_pair(pairs - 1)
     sums_in[me] = sums_out[me]
 
     @pl.loop(0, 3 * chunks)
@@ -254,13 +259,14 @@
     def _(k):
         stream_copy(0, chunk_at(k)).wait()
 
-    def rest_tile(u, t):
+    pick = lax.broadcasted_iota(jnp.int32, (BLOCK, LANES), 1) // BLOCK
+    groups = LANES // BLOCK
+
+    def filters_stage(u, t):
         lane = pl.ds(pl.multiple_of(t * LANES, LANES), LANES)
         inside = lax.broadcasted_iota(jnp.int32, (BLOCK, LANES), 1) % BLOCK
         row = lax.broadcasted_iota(jnp.int32, (BLOCK, LANES), 0)
-        pick = lax.broadcasted_iota(jnp.int32, (BLOCK, LANES), 1) // BLOCK
-        group = t * (LANES // BLOCK)
-        r, a = picked(few_rates, group, pick), picked(few_amps, group, pick)
+        r, a = picked(few_rates, t * groups, pick), picked(few_amps, t * groups, pick)
         own = row == inside
         r_own = jnp.sum(jnp.where(own, r, 0.0), axis=0, keepdims=True)
         a_own = jnp.sum(jnp.where(own, a, 0.0), axis=0, keepdims=True)
@@ -282,50 +288,70 @@
         near = halves(jnp.where(row.astype(F32) >= inside, span[:BLOCK], 0.0))
         far = halves(span[BLOCK:])
         back = halves(jnp.exp(-r * (BLOCK - 1.0 - inside)))
-        weights = stack_rows([(far[0], False), (far[1], True), (near[0], False), (back[0], False),
-                              (near[1], True), (back[1], True)])
-        shifted_rows(u, 0, t // PER_CHUNK, lax.rem(t, PER_CHUNK))
-        by_query = stream_taps(0, t)
-        step = jnp.exp(-float(BLOCK) * r)
-        state = jnp.zeros((BLOCK, LANES), F32)
+        weights[u] = stack_rows([(far[0], False), (far[1], True), (near[0], False), (back[0], False),
+                                 (near[1], True), (back[1], True)])
+
+    def near_stage(u, t):
+        lane = pl.ds(pl.multiple_of(t * LANES, LANES), LANES)
+        step = jnp.exp(-float(BLOCK) * picked(few_rates, t * groups, pick))
+        by = weights[u]
 
         def block_u(b):
             at = pl.ds(b * BLOCK, BLOCK)
             return u_high[at, lane], u_low[at, lane]
 
+        products = []
         for quad in range(blocks // 4):
-            even = jnp.dot(weights, paired(mask, block_u(4 * quad), block_u(4 * quad + 2)), preferred_element_type=F32)
-            odd = jnp.dot(weights[2 * BLOCK:], paired(mask, block_u(4 * quad + 1), block_u(4 * quad + 3)),
-                          preferred_element_type=F32)
-            states, values = [], []
-            for b in range(4):
-                side = slice((b // 2) * LANES, (b // 2 + 1) * LANES)
-                part = odd[:, side] if b % 2 else even[2 * BLOCK:, side]
-                value = loc[pl.ds((4 * quad + b) * BLOCK, BLOCK), lane] + (part[:BLOCK] + part[2 * BLOCK:3 * BLOCK])
-                if b % 2:
-                    value = value + (even[:BLOCK, side] + even[BLOCK:2 * BLOCK, side])
-                else:
-                    states.append(halves(state))
-                values.append(value)
-                state = state * step + (part[BLOCK:2 * BLOCK] + part[3 * BLOCK:])
-            both = jnp.dot(by, paired(mask, *states), preferred_element_type=F32)
-            for b in range(4):
-                value = both[:, (b // 2) * LANES:(b // 2 + 1) * LANES]
-                half = (b % 2) * BLOCK
-                total = values[b] + (value[half:half + BLOCK] + value[SPAN + half:SPAN + half + BLOCK])
-                if quad == 0 and b == 0:
-                    first_rows[t] = total[:8]
-                at = pl.ds((4 * quad + b) * BLOCK, BLOCK)
-                gate = filtered(u, by_query, 4 * quad + b)
-                query[at, lane] = gate
-                loc[at, lane] = gate * total
-
-    answered = tiles // 2
-
-    @pl.loop(0, answered, step=UNROLL)
-    def _(t):
-        for u in range(UNROLL):
-            rest_tile(u, t + u)
+            products.append((
+                jnp.dot(by, paired(mask, block_u(4 * quad), block_u(4 * quad + 2)), preferred_element_type=F32),
+                jnp.dot(by[2 * BLOCK:], paired(mask, block_u(4 * quad + 1), block_u(4 * quad + 3)),
+                        preferred_element_type=F32)))
+        state = jnp.zeros((BLOCK, LANES), F32)
+        for b in range(blocks):
+            even, odd = products[b // 4]
+            side = slice((b % 4 // 2) * LANES, (b % 4 // 2 + 1) * LANES)
+            part = odd[:, side] if b % 2 else even[2 * BLOCK:, side]
+            value = part[:BLOCK] + part[2 * BLOCK:3 * BLOCK]
+            if b % 2:
+                value = value + (even[:BLOCK, side] + even[BLOCK:2 * BLOCK, side])
+            else:
+                states[u, b // 2, 0], states[u, b // 2, 1] = halves(state)
+            loc[pl.ds(b * BLOCK, BLOCK), lane] += value
+            state = state * step + (part[BLOCK:2 * BLOCK] + part[3 * BLOCK:])
+
+    def gate_stage(u, t):
+        lane = pl.ds(pl.multiple_of(t * LANES, LANES), LANES)
+        low = forward_low[0:SPAN, lane]
+        by = stack_rows([(forward_high[0:SPAN, lane], False), (low, True)])
+        products = [jnp.dot(by, paired(mask, (states[u, m, 0], states[u, m, 1]), (states[u, m + 1, 0], states[u, m + 1, 1])),
+                            preferred_element_type=F32) for m in range(0, rows // SPAN, 2)]
+        shifted_rows(u, 0, t // PER_CHUNK, lax.rem(t, PER_CHUNK))
+        by_query = stream_taps(0, t)
+        for b in range(blocks):
+            at = pl.ds(b * BLOCK, BLOCK)
+            value = products[b // 4][:, (b % 4 // 2) * LANES:(b % 4 // 2 + 1) * LANES]
+            half = (b % 2) * BLOCK
+            total = loc[at, lane] + (value[half:half + BLOCK] + value[SPAN + half:SPAN + half + BLOCK])
+            if b == 0:
+                first_rows[t] = total[:8]
+            gate = filtered(u, by_query, b)
+            query[at, lane] = gate
+            loc[at, lane] = gate * total
+
+    def stages(i, which):
+        for stage, back in ((gate_stage, 2), (near_stage, 1), (filters_stage, 0)):
+            if back in which:
+                for u in range(UNROLL):
+                    stage(u, (i - back) * UNROLL + u)
+
+    steps = tiles // UNROLL
+    answered = steps // 2
+    stages(0, (0,))
+    stages(1, (0, 1))
+
+    @pl.loop(2, answered)
+    def _(i):
+        stages(i, (0, 1, 2))
 
     def sums_arrival(d):
         return pltpu.make_async_remote_copy(
@@ -346,8 +372,7 @@
     def _(i):
         sums_arrival(lax.rem(me + i, count)).wait_recv()
 
-    pick = lax.broadcasted_iota(jnp.int32, (BLOCK, LANES), 1) // BLOCK
-    r = picked(few_rates, me * (LANES // BLOCK), pick)
+    r = picked(few_rates, me * groups, pick)
     device_decay = jnp.exp(-float(rows) * r)
     ahead = jnp.exp(r)
     further = ahead * ahead
@@ -368,10 +393,12 @@
     def _(i):
         back_copy(lax.rem(me + i, count)).start()
 
-    @pl.loop(answered, tiles, step=UNROLL)
-    def _(t):
-        for u in range(UNROLL):
-            rest_tile(u, t + u)
+    @pl.loop(answered, steps)
+    def _(i):
+        stages(i, (0, 1, 2))
+
+    stages(steps, (1, 2))
+    stages(steps + 1, (2,))
 
     rim_copy.wait()
     has_rim = jnp.where(me > 0, 1.0, 0.0)
@@ -386,7 +413,7 @@
             first, second = rim_effect(
                 stream_taps(1, t), stream_taps(2, t), [edge[i:i + 1] for i in range(4)],
                 [rim[1][0:1], rim[1][1:2], rim[2][0:1], rim[2][1:2]])
-            r, a = picked(few_rates, t * (LANES // BLOCK), pick), picked(few_amps, t * (LANES // BLOCK), pick)
+            r, a = picked(few_rates, t * groups, pick), picked(few_amps, t * groups, pick)
             before = jnp.sum(a * jnp.exp(r), axis=0, keepdims=True)
             direct = skip[0:1, lane]
             by_query = stream_taps(0, t)
@@ -463,9 +490,11 @@
             pltpu.VMEM((rows, channels), BF16),
             pltpu.VMEM((rows, channels), BF16),
             pltpu.VMEM((tiles, 8, LANES), F32),
+            pltpu.VMEM((UNROLL, 6 * BLOCK, PAIR), BF16),
+            pltpu.VMEM((UNROLL, rows // SPAN, 2, BLOCK, LANES), BF16),
             pltpu.VMEM((3 * chunks, 8, LANES), F32),
             pltpu.VMEM((3 * chunks, 8, LANES), F32),
-            pltpu.VMEM((4, rows + 8, LANES), F32),
+            pltpu.VMEM((max(4, UNROLL), rows + 8, LANES), F32),
             pltpu.VMEM((count, BLOCK + EDGES, LANES), F32),
             pltpu.VMEM((count, BLOCK + EDGES, LANES), F32),
             pltpu.VMEM((count, BLOCK, LANES), F32),

time: 42 us -> 29.5 us (0.70)
  Pallas kernels: 41.9 us -> 29.4 us
    pallas_call x1, Pallas kernels: 39.2 us -> 26.7 us  [body(): pl.pallas_call(functools.partial(main_kernel, count), out_shape=tuple((pl...]
where the time goes in v4:
time: 29.5 us; the launch traced here: 29.4 us
  Pallas kernels  29.4 us (100%)
    pallas_call x1, Pallas kernels, body(): pl.pallas_call(functools.partial(main_kernel, count), out_shape=tuple((pl...  26.7 us
    pallas_call x1, Pallas kernels, body(): pl.pallas_call(last_kernel, out_shape=jax.ShapeDtypeStruct((rows, channel...  2.68 us

profile of v4, /device:TPU:1, one launch (start us, length us, event | category | flops | bytes accessed | tf_op | source)
XLA Modules:
  0.0 29.4 jit_solution(9041226424841099793)
XLA Ops:
  0.0 26.7 %local_part.1 = (f32[256,4096]{1,0:T(8,128)S(1)}, f32[256,4096]{1,0:T(8,128)S(1)}, bf16[256,4096]{1,0:T(8,128)(2,1)S(1)}, bf16[256,4096]{1,0:T(8,128)(2,1)S(1)}, f32[16,4096]{1,0:T(8,128)S(1)}) custom-call(bf16[256,12288]{1,0:T(8,128)(2,1)} %streams.1, f32[3,12288]{1,0:T(4,128)} %taps_in.1, f32[16,256]{1,0:T(8,128)} %bitcast.3, f32[16,256]{1,0:T(8,128)} %bitcast.4, ...), custom_call_target="tpu_custom_call" | custom-call | tf_op jit(solution)/shard_map/local_part/pallas_call | solution.py:477
  26.7 2.7 %carried_part.1 = f32[256,4096]{1,0:T(8,128)} custom-call(f32[256,4096]{1,0:T(8,128)S(1)} %get-tuple-element.10.loc, f32[256,4096]{1,0:T(8,128)S(1)} %get-tuple-element.11.query, bf16[256,4096]{1,0:T(8,128)(2,1)S(1)} %get-tuple-element.12.forward_high, bf16[256,4096]{1,0:T(8,128)(2,1)S(1)} %get-tuple-element.13.forward_low, ...), custom_call_target="tpu_custom_call" | custom-call | tf_op jit(solution)/shard_map/carried_part/pallas_call | solution.py:515

commit v5 on v4

--- a/solution.py
+++ b/solution.py
@@ -100,9 +100,6 @@
     def _(i):
         pl.semaphore_signal(barrier, inc=1, device_id={"ctx": lax.rem(me + i, count)}, device_id_type=MESH)
 
-    @pl.loop(0, chunks)
-    def _(k):
-        stream_copy(0, chunk_at(k)).start()
 
     small[0].wait()
     small[1].wait()
@@ -114,8 +111,9 @@
         part = pl.ds(pl.multiple_of(group // LANES * LANES, LANES), LANES)
         return jnp.take_along_axis(ref[:, part], index + lax.rem(group, LANES), axis=1, mode="promise_in_bounds")
 
-    @pl.loop(0, tiles // 2)
-    def _(t):
+    def backward_pair(q):
+        c, p = pair_at(q)
+        t = c * halfs + p
         zero = jnp.zeros((BLOCK, LANES), jnp.int32)
         gap = LANES - 1.0 - lax.broadcasted_iota(jnp.int32, (BLOCK, LANES), 1).astype(F32)
         for g in range(PAIR // BLOCK):
@@ -153,9 +151,12 @@
             total = total + by[tap] * shifted[slot, pl.ds(8 + BLOCK * b - tap, BLOCK), :]
         return total
 
+    def slot_rows(d):
+        return pl.ds(pl.multiple_of(d * (BLOCK + EDGES), 8), BLOCK + EDGES)
+
     def sums_copy(t):
         return pltpu.make_async_remote_copy(
-            src_ref=sums_out.at[t], dst_ref=sums_in.at[me], send_sem=sums_send.at[t], recv_sem=sums_recv.at[me],
+            src_ref=sums_out.at[t], dst_ref=sums_in.at[slot_rows(me)], send_sem=sums_send.at[t], recv_sem=sums_recv.at[me],
             device_id={"ctx": t}, device_id_type=MESH)
 
     halfs = PER_CHUNK // 2
@@ -170,6 +171,9 @@
         for side in range(2):
             j = 2 * p + side
             t = c * PER_CHUNK + j
+            for s in range(3):
+                lane = pl.ds(pl.multiple_of(s * channels + t * LANES, LANES), LANES)
+                rim_out[s * chunks + c, pl.ds(2 * j, 2), :] = last[:, lane].astype(F32)[BLOCK - 2:]
             lane = pl.ds(pl.multiple_of(t * LANES, LANES), LANES)
             at_key, at_value = 2 * side, 2 * side + 1
             shifted_rows(at_key, 1, c, j)
@@ -218,16 +222,19 @@
             c = chunk_at(q // halfs)
             stream_copy(1, c).wait()
             stream_copy(2, c).wait()
+            stream_copy(0, c).start()
 
     pairs = tiles // 2
     greeted = pairs // 2
     chunk_wait(0)
+    backward_pair(0)
     values_pair(0)
 
     @pl.loop(1, greeted)
     def _(q):
         chunk_wait(q)
         sums_pair(q - 1)
+        backward_pair(q)
         values_pair(q)
 
     pl.semaphore_wait(barrier, count - 1)
@@ -240,18 +247,13 @@
     def _(q):
         chunk_wait(q)
         sums_pair(q - 1)
+        backward_pair(q)
         values_pair(q)
         send_pair(q - 1)
 
     sums_pair(pairs - 1)
     send_pair(pairs - 1)
-    sums_in[me] = sums_out[me]
-
-    @pl.loop(0, 3 * chunks)
-    def _(e):
-        for p in range(PER_CHUNK):
-            lane = pl.ds(pl.multiple_of(e * WIDE + p * LANES, LANES), LANES)
-            rim_out[e, 2 * p:2 * p + 2, :] = last[:, lane].astype(F32)[BLOCK - 2:]
+    sums_in[slot_rows(me), :] = sums_out[me]
 
     rim_copy.start()
 
@@ -355,7 +357,7 @@
 
     def sums_arrival(d):
         return pltpu.make_async_remote_copy(
-            src_ref=sums_out.at[d], dst_ref=sums_in.at[d], send_sem=sums_send.at[d], recv_sem=sums_recv.at[d],
+            src_ref=sums_out.at[d], dst_ref=sums_in.at[slot_rows(d)], send_sem=sums_send.at[d], recv_sem=sums_recv.at[d],
             device_id={"ctx": d}, device_id_type=MESH)
 
     def back_copy(d):
@@ -377,16 +379,14 @@
     ahead = jnp.exp(r)
     further = ahead * ahead
     key_taps, value_taps = stream_taps(1, me), stream_taps(2, me)
+    edge = [sums_in[pl.ds(BLOCK + i, count, stride=BLOCK + EDGES), :] for i in range(EDGES)]
+    rim = [jnp.concatenate([jnp.zeros((1, LANES), F32), x[:-1]], axis=0) for x in edge[4:]]
+    first, second = rim_effect(key_taps, value_taps, edge[:4], rim)
     state = jnp.zeros((BLOCK, LANES), F32)
     for d in range(count):
-        if d:
-            edge = sums_in[d, BLOCK:BLOCK + EDGES]
-            rim = sums_in[d - 1, BLOCK:BLOCK + EDGES]
-            first, second = rim_effect(key_taps, value_taps, [edge[i:i + 1] for i in range(4)],
-                                       [rim[i:i + 1] for i in range(4, 8)])
-            state = state + (ahead * first + further * second)
+        state = state + (ahead * first[d:d + 1] + further * second[d:d + 1])
         back_out[d] = state
-        state = state * device_decay + sums_in[d, 0:BLOCK]
+        state = state * device_decay + sums_in[d * (BLOCK + EDGES):d * (BLOCK + EDGES) + BLOCK, :]
     back_in[me] = back_out[me]
 
     @pl.loop(1, count)
@@ -403,9 +403,10 @@
     rim_copy.wait()
     has_rim = jnp.where(me > 0, 1.0, 0.0)
 
-    @pl.loop(0, chunks)
-    def _(c):
-        for j in range(PER_CHUNK):
+    @pl.loop(0, chunks, step=2)
+    def _(two):
+        for i in range(2 * PER_CHUNK):
+            c, j = two + i // PER_CHUNK, i % PER_CHUNK
             t = c * PER_CHUNK + j
             lane = pl.ds(pl.multiple_of(t * LANES, LANES), LANES)
             rim = [rim_in[s * chunks + c, 2 * j:2 * j + 2, :] * has_rim for s in range(3)]
@@ -496,7 +497,7 @@
             pltpu.VMEM((3 * chunks, 8, LANES), F32),
             pltpu.VMEM((max(4, UNROLL), rows + 8, LANES), F32),
             pltpu.VMEM((count, BLOCK + EDGES, LANES), F32),
-            pltpu.VMEM((count, BLOCK + EDGES, LANES), F32),
+            pltpu.VMEM((count * (BLOCK + EDGES), LANES), F32),
             pltpu.VMEM((count, BLOCK, LANES), F32),
             pltpu.VMEM((count, BLOCK, LANES), F32),
             pltpu.SemaphoreType.DMA((3, chunks)),

time: 29.5 us -> 28.3 us (0.959)
  Pallas kernels: 29.4 us -> 28.1 us
    pallas_call x1, Pallas kernels: 26.7 us -> 25.4 us  [body(): pl.pallas_call(functools.partial(main_kernel, count), out_shape=tuple((pl...]
where the time goes in v5:
time: 28.3 us; the launch traced here: 28.1 us
  Pallas kernels  28.1 us (99%)
    pallas_call x1, Pallas kernels, body(): pl.pallas_call(functools.partial(main_kernel, count), out_shape=tuple((pl...  25.4 us
    pallas_call x1, Pallas kernels, body(): pl.pallas_call(last_kernel, out_shape=jax.ShapeDtypeStruct((rows, channel...  2.68 us

profile of v5, /device:TPU:1, one launch (start us, length us, event | category | flops | bytes accessed | tf_op | source)
XLA Modules:
  0.0 28.1 jit_solution(4839992678317843926)
XLA Ops:
  0.0 25.4 %local_part.1 = (f32[256,4096]{1,0:T(8,128)S(1)}, f32[256,4096]{1,0:T(8,128)S(1)}, bf16[256,4096]{1,0:T(8,128)(2,1)S(1)}, bf16[256,4096]{1,0:T(8,128)(2,1)S(1)}, f32[16,4096]{1,0:T(8,128)S(1)}) custom-call(bf16[256,12288]{1,0:T(8,128)(2,1)} %streams.1, f32[3,12288]{1,0:T(4,128)} %taps_in.1, f32[16,256]{1,0:T(8,128)} %bitcast.3, f32[16,256]{1,0:T(8,128)} %bitcast.4, ...), custom_call_target="tpu_custom_call" | custom-call | tf_op jit(solution)/shard_map/local_part/pallas_call | solution.py:478
  25.5 2.7 %carried_part.1 = f32[256,4096]{1,0:T(8,128)} custom-call(f32[256,4096]{1,0:T(8,128)S(1)} %get-tuple-element.10.loc, f32[256,4096]{1,0:T(8,128)S(1)} %get-tuple-element.11.query, bf16[256,4096]{1,0:T(8,128)(2,1)S(1)} %get-tuple-element.12.forward_high, bf16[256,4096]{1,0:T(8,128)(2,1)S(1)} %get-tuple-element.13.forward_low, ...), custom_call_target="tpu_custom_call" | custom-call | tf_op jit(solution)/shard_map/carried_part/pallas_call | solution.py:516

commit v6 on v5

--- a/solution.py
+++ b/solution.py
@@ -341,9 +341,9 @@
             loc[at, lane] = gate * total
 
     def stages(i, which):
-        for stage, back in ((gate_stage, 2), (near_stage, 1), (filters_stage, 0)):
-            if back in which:
-                for u in range(UNROLL):
+        for u in range(UNROLL):
+            for stage, back in ((gate_stage, 2), (near_stage, 1), (filters_stage, 0)):
+                if back in which:
                     stage(u, (i - back) * UNROLL + u)
 
     steps = tiles // UNROLL
@@ -403,9 +403,9 @@
     rim_copy.wait()
     has_rim = jnp.where(me > 0, 1.0, 0.0)
 
-    @pl.loop(0, chunks, step=2)
+    @pl.loop(0, chunks, step=chunks)
     def _(two):
-        for i in range(2 * PER_CHUNK):
+        for i in range(chunks * PER_CHUNK):
             c, j = two + i // PER_CHUNK, i % PER_CHUNK
             t = c * PER_CHUNK + j
             lane = pl.ds(pl.multiple_of(t * LANES, LANES), LANES)

time: 28.3 us -> 27.4 us (0.968)
  Pallas kernels: 28.1 us -> 27.2 us
    pallas_call x1, Pallas kernels: 25.4 us -> 24.5 us  [body(): pl.pallas_call(functools.partial(main_kernel, count), out_shape=tuple((pl...]
where the time goes in v6:
time: 27.4 us; the launch traced here: 27.2 us
  Pallas kernels  27.2 us (99%)
    pallas_call x1, Pallas kernels, body(): pl.pallas_call(functools.partial(main_kernel, count), out_shape=tuple((pl...  24.5 us
    pallas_call x1, Pallas kernels, body(): pl.pallas_call(last_kernel, out_shape=jax.ShapeDtypeStruct((rows, channel...  2.68 us

profile of v6, /device:TPU:1, one launch (start us, length us, event | category | flops | bytes accessed | tf_op | source)
XLA Modules:
  0.0 27.2 jit_solution(11545976047100242147)
XLA Ops:
  0.0 24.5 %local_part.1 = (f32[256,4096]{1,0:T(8,128)S(1)}, f32[256,4096]{1,0:T(8,128)S(1)}, bf16[256,4096]{1,0:T(8,128)(2,1)S(1)}, bf16[256,4096]{1,0:T(8,128)(2,1)S(1)}, f32[16,4096]{1,0:T(8,128)S(1)}) custom-call(bf16[256,12288]{1,0:T(8,128)(2,1)} %streams.1, f32[3,12288]{1,0:T(4,128)} %taps_in.1, f32[16,256]{1,0:T(8,128)} %bitcast.3, f32[16,256]{1,0:T(8,128)} %bitcast.4, ...), custom_call_target="tpu_custom_call" | custom-call | tf_op jit(solution)/shard_map/local_part/pallas_call | solution.py:478
  24.5 2.7 %carried_part.1 = f32[256,4096]{1,0:T(8,128)} custom-call(f32[256,4096]{1,0:T(8,128)S(1)} %get-tuple-element.10.loc, f32[256,4096]{1,0:T(8,128)S(1)} %get-tuple-element.11.query, bf16[256,4096]{1,0:T(8,128)(2,1)S(1)} %get-tuple-element.12.forward_high, bf16[256,4096]{1,0:T(8,128)(2,1)S(1)} %get-tuple-element.13.forward_low, ...), custom_call_target="tpu_custom_call" | custom-call | tf_op jit(solution)/shard_map/carried_part/pallas_call | solution.py:516
